TPU v7x, 32 devices: a whole 2x2x4 slice. The times are simulated.
32 devices in a mesh: row: 8 (over z, x), col: 4 (over y, core).
Axes of the slice: x: 2, y: 2, z: 4, core: 2. Of those that a mesh axis runs over, the one named last changes fastest.
Arguments:
- tile_vals: bfloat16 [8, 4, 256, 128, 128], P('row', 'col'), may hold values from -0.125 to 0.125
- tile_row: int32 [8, 4, 256], P('row', 'col'), may hold values from 0 to 15
- tile_col: int32 [8, 4, 256], P('row', 'col'), may hold values from 0 to 31
- tile_count: int32 [8, 4], P('row', 'col'), may hold values from 64 to 256
- out_grad: bfloat16 [16384, 128], P('row', 'col'), may hold values from -6 to 6
- relu_mask: int32 [16384, 128], P('row', 'col'), may hold values 0 or 1
- features: bfloat16 [16384, 128], P(('row', 'col')), may hold values from -6 to 6
- weight: bfloat16 [128, 128], replicated, may hold values from -0.5 to 0.5
- importance: float32 [128, 128], replicated, may hold values from 0 to 1
- weight_delta: float32 [128, 128], replicated, may hold values from -0.046875 to 0.046875
Outputs:
- input_grad: bfloat16 [16384, 128], P(('row', 'col'))
- importance_out: float32 [128, 128], replicated
All inputs are finite; a program needn't handle non-finite values. No bound on the sum of `relu_mask` on one device may be relied on, other than what follows from the above.
Results may differ from a plain program's by a relative error of at most 0.022.
Values may be sent and summed in bfloat16 or wider, within the bound.
A program may use at most 128 MiB of HBM per device.

v0:
```python
import jax
import jax.numpy as jnp
from jax import lax
from jax.sharding import PartitionSpec as P


def local(
    tile_vals,
    tile_row,
    tile_col,
    tile_count,
    out_grad,
    relu_mask,
    features,
    weight,
    importance,
    weight_delta,
):
    tile_side = tile_vals.shape[-1]
    slots = tile_vals.shape[2]
    node_rows = features.shape[0]
    row_devices = lax.axis_size("row")
    masked = (out_grad.astype(jnp.float32) * relu_mask.astype(jnp.float32)).astype(jnp.bfloat16)
    gathered = lax.all_gather(masked, "col", axis=1, tiled=True)
    width = gathered.shape[1]
    row_tiles = gathered.reshape(-1, tile_side, width)
    picked = jnp.take(row_tiles, tile_row.reshape(slots), axis=0)
    product = jnp.einsum(
        "tij,tif->tjf",
        tile_vals.reshape(slots, tile_side, tile_side),
        picked,
        preferred_element_type=jnp.float32,
    )
    flat_product = product.reshape(slots, tile_side * width)
    usable = lax.iota(jnp.int32, slots) < tile_count.reshape(())
    column_ids = tile_col.reshape(slots)
    row_count = node_rows * row_devices
    tile_ids = lax.iota(jnp.int32, row_count // tile_side)
    selector = ((column_ids[None, :] == tile_ids[:, None]) & usable[None, :]).astype(jnp.float32)
    summed = jnp.dot(
        selector, flat_product, precision=lax.Precision.HIGHEST, preferred_element_type=jnp.float32
    )
    partial_value = summed.reshape(row_count, width)
    aggregate = lax.psum_scatter(
        partial_value.astype(jnp.bfloat16), "row", scatter_dimension=0, tiled=True
    )
    input_grad = lax.dot_general(
        aggregate, weight, (((1,), (1,)), ((), ())), preferred_element_type=jnp.float32
    ).astype(jnp.bfloat16)
    local_grad = lax.dot_general(
        features, aggregate, (((0,), (0,)), ((), ())), preferred_element_type=jnp.float32
    )
    weight_grad = lax.psum(local_grad, ("row", "col"))
    importance_out = importance - weight_grad * weight_delta
    return (input_grad, importance_out)


def solution(mesh):
    return jax.shard_map(
        local,
        mesh=mesh,
        in_specs=(
            P("row", "col", None, None, None),
            P("row", "col", None),
            P("row", "col", None),
            P("row", "col"),
            P("row", "col"),
            P("row", "col"),
            P(("row", "col"), None),
            P(),
            P(),
            P(),
        ),
        out_specs=(P(("row", "col"), None), P()),
        check_vma=False,
    )
```

profile of v0, /device:TPU:0, one launch (start us, length us, event | category | flops | bytes accessed | tf_op | source)
XLA Modules:
  0.0 269.2 jit_solution(76802143404267823)
XLA Ops:
  7.2 0.0 copy-start
  7.2 0.0 reduce-scatter.2.cloned.1.call-start
  7.2 1.0 multiply_convert_fusion
  8.3 8.6 %all_gather.3 = bf16[2048,128]{0,1:T(8,128)(2,1)S(1)} all-gather(bf16[2048,32]{0,1:T(8,128)(2,1)S(1)} %multiply_convert_fusion), channel_id=1, replica_groups=mesh['row'=8,'col'=4] {'col'}, dimensions={1}, use_global_device_ids=true | all-gather | bytes 655360 | tf_op jit(solution)/shard_map/all_gather | solution.py:24
  16.9 0.3 copy.15
  17.2 0.7 compare_select_fusion
  17.9 0.7 compare_and_fusion
  18.6 8.6 %gather_fusion = bf16[256,128,128]{2,1,0:T(8,128)(2,1)} fusion(bf16[16,128,128]{2,1,0:T(8,128)(2,1)S(1)} %bitcast.21, s32[1024]{0:T(1024)S(1)} %pad_clamp_fusion), kind=kCustom, calls=%fused_computation | custom fusion | bytes 16778240 | tf_op jit(solution)/shard_map/jit(_take)/gather | solution.py:27
  27.2 14.7 %convolution_bitcast_fusion = f32[256,128,128]{1,2,0:T(8,128)} fusion(bf16[1,1,256,128,128]{4,3,2,1,0:T(8,128)(2,1)} %param.10, bf16[256,128,128]{2,1,0:T(8,128)(2,1)} %gather_fusion, pred[256]{0:T(512)(128)(4,1)S(1)} %compare_and_fusion), kind=kOutput, calls=%fused_computation.2 | convolution fusion | flops 1077936128 | bytes 33554688 | tf_op jit(solution)/shard_map/tij,tif->tjf/dot_general | solution.py:28
  41.8 17.8 %copy.17 = f32[256,128,128]{0,2,1:T(8,128)} copy(f32[256,128,128]{1,2,0:T(8,128)} %convolution_bitcast_fusion) | data formatting | bytes 33554432 | tf_op jit(solution)/shard_map/tij,tif->tjf/dot_general | solution.py:28
  60.3 0.0 copy-start.3
  60.3 11.0 %convolution_convert_fusion = bf16[32,16384]{1,0:T(8,128)(2,1)S(1)} fusion(f32[256,16384]{0,1:T(8,128)} %bitcast.22, s32[256]{0:T(256)S(1)} %bitcast.23, pred[256]{0:T(512)(128)(4,1)S(1)} %iota_compare_fusion.1), kind=kOutput, calls=%fused_computation.1 | convolution fusion | flops 1611153408 | bytes 17827072 | tf_op jit(solution)/shard_map/dot_general | solution.py:40
  71.3 1.3 convert_element_type.23
  72.6 0.0 reduce-scatter.2.cloned.1.call-update
  72.6 0.0 all-reduce.2.cloned.1.call-start
  72.7 0.1 copy.18
  72.8 0.1 copy.19
  72.9 64.2 %reduce-scatter.2.cloned.1.call-done = bf16[512,128]{1,0:T(8,128)(2,1)} async-done(((bf16[4096,128]{1,0:T(8,128)(2,1)}), bf16[512,128]{1,0:T(8,128)(2,1)}) %reduce-scatter.2.cloned.1.call-update) | async-done | bytes 131088 | tf_op jit(solution)/shard_map/reduce_scatter | solution.py:44
  137.1 1.8 convolution_bitcast_fusion.1
  138.9 0.0 all-reduce.2.cloned.1.call-update
  138.9 1.8 convolution_convert_fusion.1
  140.6 120.1 %all-reduce.2.cloned.1.call-done = f32[128,128]{0,1:T(8,128)} async-done(((f32[128,128]{0,1:T(8,128)}), f32[128,128]{0,1:T(8,128)}) %all-reduce.2.cloned.1.call-update) | async-done | bytes 65552 | tf_op jit(solution)/shard_map/psum | solution.py:53
  260.8 0.9 multiply_subtract_fusion
  261.6 0.7 copy.20
  (10 shorter events, 0.0 us)
Async XLA Ops:
  7.2 129.9 %copy-start = (bf16[512,128]{1,0:T(8,128)(2,1)S(1)}, bf16[512,128]{1,0:T(8,128)(2,1)}, u32[]{:S(2)}) copy-start(bf16[512,128]{1,0:T(8,128)(2,1)} %param.16) | copy-start | bytes 393220
  7.2 129.9 %reduce-scatter.2.cloned.1.call-start = ((), (), s32[]{:S(2)}) async-start(), calls=%async_computation.1 | async-start | bytes 1179648 | tf_op jit(solution)/shard_map/reduce_scatter | solution.py:44
  41.8 18.5 %copy-start.4 = (s32[1,1,256]{2,1,0:T(1,128)S(1)}, s32[1,1,256]{2,1,0:T(1,128)}, u32[]{:S(2)}) copy-start(s32[1,1,256]{2,1,0:T(1,128)} %param.12) | copy-start | bytes 3076
  60.3 12.4 %copy-start.1 = (f32[128,128]{1,0:T(8,128)S(1)}, f32[128,128]{1,0:T(8,128)}, u32[]{:S(2)}) copy-start(f32[128,128]{1,0:T(8,128)} %param.19) | copy-start | bytes 196612
  60.3 12.5 %copy-start.2 = (f32[128,128]{1,0:T(8,128)S(1)}, f32[128,128]{1,0:T(8,128)}, u32[]{:S(2)}) copy-start(f32[128,128]{1,0:T(8,128)} %param.18) | copy-start | bytes 196612
  60.3 78.6 %copy-start.3 = (bf16[128,128]{1,0:T(8,128)(2,1)S(1)}, bf16[128,128]{1,0:T(8,128)(2,1)}, u32[]{:S(2)}) copy-start(bf16[128,128]{1,0:T(8,128)(2,1)} %param.17) | copy-start | bytes 98308
  72.6 188.2 %all-reduce.2.cloned.1.call-start = ((), (), s32[]{:S(2)}) async-start(), calls=%async_computation.2 | async-start | bytes 131072 | tf_op jit(solution)/shard_map/psum | solution.py:53
Sparse Core Ops, SparseCore 0:
  72.7 64.3 reduce-scatter.1
  144.2 116.5 all-reduce.1
where the time goes:
time: 271 us; the launch traced here: 269 us
  waiting for transfers between devices  184 us (68%)
  matrix products  29.1 us (11%)
  local copies, waits for them, and re-layouts  28.9 us (11%)
  between operations  14.8 us (5%)
  blocking collectives  8.65 us (3%)
  other arithmetic  3.28 us (1%)
    psum x1, waiting for transfers between devices, local(): weight_grad = lax.psum(local_grad, ('row', 'col'))  120 us
    reduce_scatter x1, waiting for transfers between devices, local(): lax.psum_scatter(partial_value.astype(jnp.bfloat16), 'row', scatter_dimen...  64.2 us
    dot_general x1, local copies, waits for them, and re-layouts, local(): jnp.einsum('tij,tif->tjf', tile_vals.reshape(slots, tile_side, tile_side)...  17.8 us
    dot_general x1, matrix products, local(): jnp.einsum('tij,tif->tjf', tile_vals.reshape(slots, tile_side, tile_side)...  14.7 us
    dot_general x1, matrix products, local(): jnp.dot(selector, flat_product, precision=lax.Precision.HIGHEST, preferre...  11 us
    all_gather x1, blocking collectives, local(): gathered = lax.all_gather(masked, 'col', axis=1, tiled=True)  8.65 us
    gather x1, local copies, waits for them, and re-layouts, local(): picked = jnp.take(row_tiles, tile_row.reshape(slots), axis=0)  8.59 us
  transfers between devices with their start and end apart: 2, of which 2 were waited for; matrix products, arithmetic and copies ran while one was open for 1% of the time, Pallas kernels for 0%

commit v1 on v0

v1 whole, which is shorter than its diff:
```python
import functools

import jax
import jax.numpy as jnp
from jax import lax
from jax.experimental import pallas as pl
from jax.experimental.pallas import tpu as pltpu
from jax.sharding import PartitionSpec as P

MESH = pl.DeviceIdType.MESH
VMEM = pl.BlockSpec(memory_space=pltpu.VMEM)
SMEM = pl.BlockSpec(memory_space=pltpu.SMEM)


def remote(src, dst, send_sem, recv_sem, device):
    return pltpu.make_async_remote_copy(
        src_ref=src,
        dst_ref=dst,
        send_sem=send_sem,
        recv_sem=recv_sem,
        device_id=device,
        device_id_type=MESH,
    )


def greet(devices):
    barrier = pltpu.get_barrier_semaphore()
    for device in devices:
        pl.semaphore_signal(barrier, inc=1, device_id=device, device_id_type=MESH)
    pl.semaphore_wait(barrier, len(devices))


def others(me, count):
    return [lax.rem(me + step, count) for step in range(1, count)]


def gather_kernel(cols, grad_ref, mask_ref, out_ref, send_sem, recv_sem):
    row, col = lax.axis_index("row"), lax.axis_index("col")
    out_ref[col] = (
        grad_ref[...].astype(jnp.float32) * mask_ref[...].astype(jnp.float32)
    ).astype(jnp.bfloat16)
    greet([(row, peer) for peer in others(col, cols)])
    sends = []
    for peer in others(col, cols):
        copy = remote(
            out_ref.at[col], out_ref.at[col], send_sem.at[peer], recv_sem.at[col], (row, peer)
        )
        copy.start()
        sends.append(copy)
    for peer in others(col, cols):
        remote(
            out_ref.at[peer], out_ref.at[peer], send_sem.at[peer], recv_sem.at[peer], (row, peer)
        ).wait_recv()
    for copy in sends:
        copy.wait_send()


def tiles_kernel(chunk, rows_ref, cols_ref, count_ref, masked_ref, vals_ref, out_ref, held, total, sems):
    slots, side = vals_ref.shape[0], vals_ref.shape[-1]
    columns = total.shape[0] - 1
    per_block = out_ref.shape[2] // side

    def fetch(index):
        part = pl.ds(index * chunk, chunk)
        return pltpu.make_async_copy(vals_ref.at[part], held.at[part], sems.at[index])

    for index in range(slots // chunk):
        fetch(index).start()
    total[...] = jnp.zeros_like(total)
    count = count_ref[0]

    @pl.loop(0, slots // chunk)
    def _(index):
        fetch(index).wait()

        @pl.when(index * chunk < count)
        def _():
            for step in range(chunk):
                tile = index * chunk + step
                start = pl.multiple_of(rows_ref[tile] * side, side)
                place = jnp.where(tile < count, cols_ref[tile], columns)
                total[place] += jnp.dot(
                    masked_ref[:, pl.ds(start, side)], held[tile], preferred_element_type=jnp.float32
                )

    for column in range(columns):
        block, part = divmod(column, per_block)
        out_ref[block, :, part * side : (part + 1) * side] = total[column].astype(jnp.bfloat16)


def reduce_kernel(
    outer,
    inner,
    cols,
    part_ref,
    feat_ref,
    weight_ref,
    imp_ref,
    delta_ref,
    grad_ref,
    imp_out_ref,
    pair_recv,
    pair_sum,
    line_recv,
    local_grad,
    col_recv,
    row_recv,
    whole_grad,
    pair_send_sem,
    pair_recv_sem,
    line_send_sem,
    line_recv_sem,
    col_send_sem,
    col_recv_sem,
    row_send_sem,
    row_recv_sem,
    all_send_sem,
    all_recv_sem,
):
    row, col = lax.axis_index("row"), lax.axis_index("col")
    rows = outer * inner
    my_outer, my_inner = lax.div(row, inner), lax.rem(row, inner)
    greet(
        [(peer, col) for peer in others(row, rows)] + [(row, peer) for peer in others(col, cols)]
    )
    sends = []

    def start(copy):
        copy.start()
        sends.append(copy)

    def arrived(slot, sem):
        remote(slot, slot, sem, sem, (row, col)).wait_recv()

    order = others(my_outer, outer) + [my_outer]
    for block in order:
        for peer in others(my_inner, inner):
            start(
                remote(
                    part_ref.at[block * inner + peer],
                    pair_recv.at[my_inner, block],
                    pair_send_sem.at[peer, block],
                    pair_recv_sem.at[my_inner, block],
                    (my_outer * inner + peer, col),
                )
            )
    value = None
    for block in order:
        value = part_ref[block * inner + my_inner].astype(jnp.float32)
        for peer in others(my_inner, inner):
            arrived(pair_recv.at[peer, block], pair_recv_sem.at[peer, block])
            value += pair_recv[peer, block].astype(jnp.float32)
        if block is not my_outer:
            pair_sum[block] = value.astype(jnp.bfloat16)
            start(
                remote(
                    pair_sum.at[block],
                    line_recv.at[my_outer],
                    line_send_sem.at[block],
                    line_recv_sem.at[my_outer],
                    (block * inner + my_inner, col),
                )
            )
    for peer in others(my_outer, outer):
        arrived(line_recv.at[peer], line_recv_sem.at[peer])
        value += line_recv[peer].astype(jnp.float32)
    aggregate = value.astype(jnp.bfloat16)

    local_grad[...] = jnp.dot(
        aggregate, feat_ref[...], preferred_element_type=jnp.float32
    ).T
    piece = local_grad.shape[0] // cols

    def rows_of(ref, index):
        return ref.at[pl.ds(pl.multiple_of(index * piece, piece), piece)]

    for peer in others(col, cols):
        start(
            remote(
                rows_of(local_grad, peer),
                col_recv.at[col],
                col_send_sem.at[peer],
                col_recv_sem.at[col],
                (row, peer),
            )
        )
    grad_ref[...] = (
        jnp.dot(weight_ref[...], aggregate, preferred_element_type=jnp.float32)
        .T.astype(jnp.bfloat16)
    )
    piece_sum = rows_of(local_grad, col)[...]
    for peer in others(col, cols):
        arrived(col_recv.at[peer], col_recv_sem.at[peer])
        piece_sum += col_recv[peer]
    row_recv[row] = piece_sum
    for peer in others(row, rows):
        start(
            remote(
                row_recv.at[row],
                row_recv.at[row],
                row_send_sem.at[peer],
                row_recv_sem.at[row],
                (peer, col),
            )
        )
    for peer in others(row, rows):
        arrived(row_recv.at[peer], row_recv_sem.at[peer])
    piece_sum = row_recv[0]
    for index in range(1, rows):
        piece_sum += row_recv[index]
    rows_of(whole_grad, col)[...] = piece_sum
    for peer in others(col, cols):
        start(
            remote(
                rows_of(whole_grad, col),
                rows_of(whole_grad, col),
                all_send_sem.at[peer],
                all_recv_sem.at[col],
                (row, peer),
            )
        )
    for peer in others(col, cols):
        arrived(rows_of(whole_grad, peer), all_recv_sem.at[peer])
    imp_out_ref[...] = imp_ref[...] - whole_grad[...] * delta_ref[...]
    for copy in sends:
        copy.wait_send()


def local(
    rows,
    cols,
    tile_vals,
    tile_row,
    tile_col,
    tile_count,
    out_grad,
    relu_mask,
    features,
    weight,
    importance,
    weight_delta,
):
    slots, side = tile_vals.shape[2], tile_vals.shape[-1]
    nodes, depth = features.shape
    block_nodes, own_width = out_grad.shape
    width = own_width * cols
    columns = rows * nodes // side
    inner = 2 if rows % 2 == 0 else 1
    outer = rows // inner
    chunk = 16
    params = functools.partial(pltpu.CompilerParams, vmem_limit_bytes=48 * 2**20)
    dma = pltpu.SemaphoreType.DMA

    masked = pl.pallas_call(
        functools.partial(gather_kernel, cols),
        out_shape=jax.ShapeDtypeStruct((cols, own_width, block_nodes), jnp.bfloat16),
        in_specs=[VMEM] * 2,
        out_specs=VMEM,
        scratch_shapes=[dma((cols,)), dma((cols,))],
        compiler_params=params(collective_id=0, has_side_effects=True),
        name="gather_masked",
    )(out_grad.T, relu_mask.T)

    partial_value = pl.pallas_call(
        functools.partial(tiles_kernel, chunk),
        out_shape=jax.ShapeDtypeStruct((rows, width, nodes), jnp.bfloat16),
        in_specs=[SMEM, SMEM, SMEM, VMEM, pl.BlockSpec(memory_space=pl.ANY)],
        out_specs=VMEM,
        scratch_shapes=[
            pltpu.VMEM((slots, side, side), jnp.bfloat16),
            pltpu.VMEM((columns + 1, width, side), jnp.float32),
            dma((slots // chunk,)),
        ],
        compiler_params=params(),
        name="tile_products",
    )(
        tile_row.reshape(slots),
        tile_col.reshape(slots),
        tile_count.reshape(1),
        masked.reshape(width, block_nodes),
        tile_vals.reshape(slots, side, side),
    )

    piece = depth // cols
    return pl.pallas_call(
        functools.partial(reduce_kernel, outer, inner, cols),
        out_shape=(
            jax.ShapeDtypeStruct((nodes, depth), jnp.bfloat16),
            jax.ShapeDtypeStruct((depth, width), jnp.float32),
        ),
        in_specs=[VMEM] * 5,
        out_specs=(VMEM, VMEM),
        scratch_shapes=[
            pltpu.VMEM((inner, outer, width, nodes), jnp.bfloat16),
            pltpu.VMEM((outer, width, nodes), jnp.bfloat16),
            pltpu.VMEM((outer, width, nodes), jnp.bfloat16),
            pltpu.VMEM((depth, width), jnp.float32),
            pltpu.VMEM((cols, piece, width), jnp.float32),
            pltpu.VMEM((rows, piece, width), jnp.float32),
            pltpu.VMEM((depth, width), jnp.float32),
            dma((inner, outer)),
            dma((inner, outer)),
            dma((outer,)),
            dma((outer,)),
            dma((cols,)),
            dma((cols,)),
            dma((rows,)),
            dma((rows,)),
            dma((cols,)),
            dma((cols,)),
        ],
        compiler_params=params(collective_id=1, has_side_effects=True),
        name="reduce_and_update",
    )(partial_value, features, weight, importance, weight_delta)


def solution(mesh):
    return jax.shard_map(
        functools.partial(local, mesh.shape["row"], mesh.shape["col"]),
        mesh=mesh,
        in_specs=(
            P("row", "col", None, None, None),
            P("row", "col", None),
            P("row", "col", None),
            P("row", "col"),
            P("row", "col"),
            P("row", "col"),
            P(("row", "col"), None),
            P(),
            P(),
            P(),
        ),
        out_specs=(P(("row", "col"), None), P()),
        check_vma=False,
    )
```

time: 271 us -> 54.5 us (0.20)
  waiting for transfers between devices: 184 us -> 0 us
  Pallas kernels: 0 us -> 48.8 us
  matrix products: 29.1 us -> 0 us
  local copies, waits for them, and re-layouts: 28.9 us -> 4.5 us
  between operations: 14.8 us -> 1.36 us
  blocking collectives: 8.65 us -> 0 us
  other arithmetic: 3.28 us -> 0 us
    psum x1 -> x0, waiting for transfers between devices: 120 us -> none  [local(): weight_grad = lax.psum(local_grad, ('row', 'col'))]
    reduce_scatter x1 -> x0, waiting for transfers between devices: 64.2 us -> none  [local(): lax.psum_scatter(partial_value.astype(jnp.bfloat16), 'row', scatter_dimen...]
    pallas_call x0 -> x3, Pallas kernels: none -> 48.8 us  [the longest x1 35.3 us: local(): pl.pallas_call(functools.partial(reduce_kernel, outer, inner, cols), out_...]
    dot_general x4 -> x0, matrix products: 29.1 us -> none  [the longest x1 14.7 us: local(): jnp.einsum('tij,tif->tjf', tile_vals.reshape(slots, tile_side, tile_side)...]
    dot_general x1 -> x0, local copies, waits for them, and re-layouts: 17.8 us -> none  [local(): jnp.einsum('tij,tif->tjf', tile_vals.reshape(slots, tile_side, tile_side)...]
    all_gather x1 -> x0, blocking collectives: 8.65 us -> none  [local(): gathered = lax.all_gather(masked, 'col', axis=1, tiled=True)]
    gather x1 -> x0, local copies, waits for them, and re-layouts: 8.59 us -> none  [local(): picked = jnp.take(row_tiles, tile_row.reshape(slots), axis=0)]
    unnamed x13 -> x18, local copies, waits for them, and re-layouts: 0.94 us -> 4.5 us
  transfers between devices with their start and end apart: 2 -> 0, of which waited for: 2 -> 0; matrix products, arithmetic and copies ran while one was open for 1% -> 0% of each run, Pallas kernels for 0% -> 0%
where the time goes in v1:
time: 54.5 us; the launch traced here: 54.6 us
  Pallas kernels  48.8 us (90%)
  local copies, waits for them, and re-layouts  4.5 us (8%)
  between operations  1.36 us (2%)
    pallas_call x1, Pallas kernels, local(): pl.pallas_call(functools.partial(reduce_kernel, outer, inner, cols), out_...  35.3 us
    pallas_call x1, Pallas kernels, local(): pl.pallas_call(functools.partial(gather_kernel, cols), out_shape=jax.Shap...  9.24 us
    unnamed x18, local copies, waits for them, and re-layouts  4.5 us
    pallas_call x1, Pallas kernels, local(): pl.pallas_call(functools.partial(tiles_kernel, chunk), out_shape=jax.Shap...  4.23 us

profile of v1, /device:TPU:0, one launch (start us, length us, event | category | flops | bytes accessed | tf_op | source)
XLA Modules:
  0.0 54.6 jit_solution(3485404573445498207)
XLA Ops:
  1.3 0.0 copy-start
  1.3 0.9 %copy-done = s32[2048,32]{0,1:T(8,128)S(1)} copy-done((s32[2048,32]{0,1:T(8,128)S(1)}, s32[2048,32]{0,1:T(8,128)}, u32[]{:S(2)}) %copy-start) | copy-done | bytes 262168
  2.2 0.0 copy-start.1
  2.2 0.9 %copy-done.1 = bf16[2048,32]{0,1:T(8,128)(2,1)S(1)} copy-done((bf16[2048,32]{0,1:T(8,128)(2,1)S(1)}, bf16[2048,32]{0,1:T(8,128)(2,1)}, u32[]{:S(2)}) %copy-start.1) | copy-done | bytes 131096
  3.1 0.0 copy-start.2
  3.1 0.0 copy-start.3
  3.1 0.0 copy-start.4
  3.1 0.0 copy-start.5
  3.1 9.2 %gather_masked.1 = bf16[4,32,2048]{2,1,0:T(8,128)(2,1)S(1)} custom-call(bf16[32,2048]{1,0:T(8,128)(2,1)S(1)} %bitcast.10, s32[32,2048]{1,0:T(8,128)S(1)} %bitcast.9), custom_call_target="tpu_custom_call" | custom-call | tf_op jit(solution)/shard_map/gather_masked/pallas_call | solution.py:254
  12.4 0.0 copy-start.6
  12.4 0.7 %copy-done.6 = s32[1,1,256]{2,1,0:T(1,128)S(1)} copy-done((s32[1,1,256]{2,1,0:T(1,128)S(1)}, s32[1,1,256]{2,1,0:T(1,128)}, u32[]{:S(2)}) %copy-start.6) | copy-done | bytes 1048
  13.1 0.0 copy-start.7
  13.1 0.7 %copy-done.7 = s32[1,1,256]{2,1,0:T(1,128)S(1)} copy-done((s32[1,1,256]{2,1,0:T(1,128)S(1)}, s32[1,1,256]{2,1,0:T(1,128)}, u32[]{:S(2)}) %copy-start.7) | copy-done | bytes 1048
  13.8 4.2 %tile_products.1.part_ref = bf16[8,128,512]{2,1,0:T(8,128)(2,1)S(1)} custom-call(s32[256]{0:T(256)S(1)} %bitcast.11, s32[256]{0:T(256)S(1)} %bitcast.12, s32[1]{0:T(128)} %bitcast.7.count_ref, bf16[128,2048]{1,0:T(8,128)(2,1)S(1)} %bitcast.8, bf16[256,128,128]{2,1,0:T(8,128)(2,1)} %bitcast.13), custom_call_target="tpu_custom_call" | custom-call | tf_op jit(solution)/shard_map/tile_products/pallas_call | solution.py:264
  18.0 0.0 copy-done.2
  18.0 0.0 copy-done.3
  18.0 0.0 copy-done.4
  18.0 0.0 copy-done.5
  18.0 35.3 %reduce_and_update.1 = (bf16[512,128]{1,0:T(8,128)(2,1)S(1)}, f32[128,128]{1,0:T(8,128)S(1)}) custom-call(bf16[8,128,512]{2,1,0:T(8,128)(2,1)S(1)} %tile_products.1.part_ref, bf16[512,128]{1,0:T(8,128)(2,1)S(1)} %copy-done.2, bf16[128,128]{1,0:T(8,128)(2,1)S(1)} %copy-done.5, f32[128,128]{1,0:T(8,128)S(1)} %copy-done.3, f32[128,128]{1,0:T(8,128)S(1)} %copy-done.4), custom_call_target="tpu_custom_call" | custom-call | tf_op jit(solution)/shard_map/reduce_and_update/pallas_call | solution.py:285
  53.3 0.7 %copy.15 = bf16[512,128]{1,0:T(8,128)(2,1)} copy(bf16[512,128]{1,0:T(8,128)(2,1)S(1)} %get-tuple-element.4) | data formatting | bytes 262144
  54.0 0.6 %copy.16 = f32[128,128]{1,0:T(8,128)} copy(f32[128,128]{1,0:T(8,128)S(1)} %get-tuple-element.5) | data formatting | bytes 131072
Async XLA Ops:
  1.3 1.0 %copy-start = (s32[2048,32]{0,1:T(8,128)S(1)}, s32[2048,32]{0,1:T(8,128)}, u32[]{:S(2)}) copy-start(s32[2048,32]{0,1:T(8,128)} %param.15) | copy-start | bytes 786436
  2.2 0.9 %copy-start.1 = (bf16[2048,32]{0,1:T(8,128)(2,1)S(1)}, bf16[2048,32]{0,1:T(8,128)(2,1)}, u32[]{:S(2)}) copy-start(bf16[2048,32]{0,1:T(8,128)(2,1)} %param.14) | copy-start | bytes 393220
  3.1 14.9 %copy-start.2 = (bf16[512,128]{1,0:T(8,128)(2,1)S(1)}, bf16[512,128]{1,0:T(8,128)(2,1)}, u32[]{:S(2)}) copy-start(bf16[512,128]{1,0:T(8,128)(2,1)} %feat_ref.1) | copy-start | bytes 393220
  3.1 14.9 %copy-start.3 = (f32[128,128]{1,0:T(8,128)S(1)}, f32[128,128]{1,0:T(8,128)}, u32[]{:S(2)}) copy-start(f32[128,128]{1,0:T(8,128)} %imp_ref.1) | copy-start | bytes 196612
  3.1 14.9 %copy-start.4 = (f32[128,128]{1,0:T(8,128)S(1)}, f32[128,128]{1,0:T(8,128)}, u32[]{:S(2)}) copy-start(f32[128,128]{1,0:T(8,128)} %delta_ref.1) | copy-start | bytes 196612
  3.1 14.9 %copy-start.5 = (bf16[128,128]{1,0:T(8,128)(2,1)S(1)}, bf16[128,128]{1,0:T(8,128)(2,1)}, u32[]{:S(2)}) copy-start(bf16[128,128]{1,0:T(8,128)(2,1)} %weight_ref.1) | copy-start | bytes 98308
  12.4 0.7 %copy-start.6 = (s32[1,1,256]{2,1,0:T(1,128)S(1)}, s32[1,1,256]{2,1,0:T(1,128)}, u32[]{:S(2)}) copy-start(s32[1,1,256]{2,1,0:T(1,128)} %param.11) | copy-start | bytes 3076
  13.1 0.7 %copy-start.7 = (s32[1,1,256]{2,1,0:T(1,128)S(1)}, s32[1,1,256]{2,1,0:T(1,128)}, u32[]{:S(2)}) copy-start(s32[1,1,256]{2,1,0:T(1,128)} %param.12) | copy-start | bytes 3076

commit v2 on v1

--- a/solution.py
+++ b/solution.py
@@ -8,8 +8,8 @@
 from jax.sharding import PartitionSpec as P
 
 MESH = pl.DeviceIdType.MESH
-VMEM = pl.BlockSpec(memory_space=pltpu.VMEM)
 SMEM = pl.BlockSpec(memory_space=pltpu.SMEM)
+HBM = pl.BlockSpec(memory_space=pltpu.HBM)
 
 
 def remote(src, dst, send_sem, recv_sem, device):
@@ -34,28 +34,107 @@
     return [lax.rem(me + step, count) for step in range(1, count)]
 
 
-def gather_kernel(cols, grad_ref, mask_ref, out_ref, send_sem, recv_sem):
+def mate_of(index):
+    return index + 1 - 2 * lax.rem(index, 2)
+
+
+def gather_kernel(
+    cols,
+    parts,
+    grad_hbm,
+    mask_hbm,
+    out_ref,
+    grad_ref,
+    mask_ref,
+    own_ref,
+    load_sem,
+    store_sem,
+    send_sem,
+    pass_sem,
+    recv_sem,
+):
     row, col = lax.axis_index("row"), lax.axis_index("col")
-    out_ref[col] = (
-        grad_ref[...].astype(jnp.float32) * mask_ref[...].astype(jnp.float32)
-    ).astype(jnp.bfloat16)
-    greet([(row, peer) for peer in others(col, cols)])
+    loads = [
+        pltpu.make_async_copy(grad_hbm, grad_ref, load_sem.at[0]),
+        pltpu.make_async_copy(mask_hbm, mask_ref, load_sem.at[1]),
+    ]
+    for load in loads:
+        load.start()
+    mate = mate_of(col)
+    far = [lax.rem(col + 2 * step, cols) for step in range(1, cols // 2)]
+    greet([(row, peer) for peer in [mate] + far])
+    for load in loads:
+        load.wait()
+    size = out_ref.shape[2] // parts
     sends = []
-    for peer in others(col, cols):
+
+    def piece(block, part):
+        return out_ref.at[block, :, part * size : (part + 1) * size]
+
+    def send(part, peer):
         copy = remote(
-            out_ref.at[col], out_ref.at[col], send_sem.at[peer], recv_sem.at[col], (row, peer)
+            own_ref.at[:, part * size : (part + 1) * size],
+            piece(col, part),
+            send_sem.at[peer, part],
+            recv_sem.at[col, part],
+            (row, peer),
         )
         copy.start()
         sends.append(copy)
-    for peer in others(col, cols):
-        remote(
-            out_ref.at[peer], out_ref.at[peer], send_sem.at[peer], recv_sem.at[peer], (row, peer)
-        ).wait_recv()
+
+    def arrived(block, part):
+        ref = piece(block, part)
+        sem = recv_sem.at[block, part]
+        remote(ref, ref, sem, sem, (row, mate)).wait_recv()
+
+    for part in range(parts):
+        lanes = slice(part * size, (part + 1) * size)
+        own_ref[:, lanes] = (
+            grad_ref[:, lanes].astype(jnp.float32) * mask_ref[:, lanes].astype(jnp.float32)
+        ).astype(jnp.bfloat16)
+        for peer in far:
+            send(part, peer)
+    for part in range(parts):
+        send(part, mate)
+    store = pltpu.make_async_copy(own_ref, out_ref.at[col], store_sem.at[0])
+    store.start()
+    for part in range(parts):
+        for peer in far:
+            arrived(peer, part)
+            ref = piece(peer, part)
+            copy = remote(
+                ref, ref, pass_sem.at[peer, part], recv_sem.at[peer, part], (row, mate)
+            )
+            copy.start()
+            sends.append(copy)
+    for part in range(parts):
+        arrived(mate, part)
+    for part in range(parts):
+        for peer in far:
+            arrived(mate_of(peer), part)
+    store.wait()
     for copy in sends:
         copy.wait_send()
 
 
-def tiles_kernel(chunk, rows_ref, cols_ref, count_ref, masked_ref, vals_ref, out_ref, held, total, sems):
+def tiles_kernel(
+    chunk,
+    rows_hbm,
+    cols_hbm,
+    count_ref,
+    masked_hbm,
+    vals_ref,
+    out_hbm,
+    held,
+    total,
+    rows_ref,
+    cols_ref,
+    masked_ref,
+    out_ref,
+    sems,
+    load_sem,
+    store_sem,
+):
     slots, side = vals_ref.shape[0], vals_ref.shape[-1]
     columns = total.shape[0] - 1
     per_block = out_ref.shape[2] // side
@@ -64,10 +143,19 @@
         part = pl.ds(index * chunk, chunk)
         return pltpu.make_async_copy(vals_ref.at[part], held.at[part], sems.at[index])
 
+    loads = [
+        pltpu.make_async_copy(rows_hbm, rows_ref, load_sem.at[0]),
+        pltpu.make_async_copy(cols_hbm, cols_ref, load_sem.at[1]),
+        pltpu.make_async_copy(masked_hbm, masked_ref, load_sem.at[2]),
+    ]
+    for load in loads:
+        load.start()
     for index in range(slots // chunk):
         fetch(index).start()
     total[...] = jnp.zeros_like(total)
-    count = count_ref[0]
+    for load in loads:
+        load.wait()
+    count = count_ref[0, 0]
 
     @pl.loop(0, slots // chunk)
     def _(index):
@@ -77,21 +165,35 @@
         def _():
             for step in range(chunk):
                 tile = index * chunk + step
-                start = pl.multiple_of(rows_ref[tile] * side, side)
-                place = jnp.where(tile < count, cols_ref[tile], columns)
+                start = pl.multiple_of(rows_ref[0, tile] * side, side)
+                place = jnp.where(tile < count, cols_ref[0, tile], columns)
                 total[place] += jnp.dot(
                     masked_ref[:, pl.ds(start, side)], held[tile], preferred_element_type=jnp.float32
                 )
 
+    stores = []
     for column in range(columns):
         block, part = divmod(column, per_block)
         out_ref[block, :, part * side : (part + 1) * side] = total[column].astype(jnp.bfloat16)
+        if part == per_block - 1:
+            store = pltpu.make_async_copy(out_ref.at[block], out_hbm.at[block], store_sem.at[block])
+            store.start()
+            stores.append(store)
+    for store in stores:
+        store.wait()
 
 
 def reduce_kernel(
     outer,
     inner,
     cols,
+    part_hbm,
+    feat_hbm,
+    weight_hbm,
+    imp_hbm,
+    delta_hbm,
+    grad_hbm,
+    imp_out_hbm,
     part_ref,
     feat_ref,
     weight_ref,
@@ -99,6 +201,9 @@
     delta_ref,
     grad_ref,
     imp_out_ref,
+    load_sem,
+    part_sem,
+    store_sem,
     pair_recv,
     pair_sum,
     line_recv,
@@ -120,6 +225,20 @@
     row, col = lax.axis_index("row"), lax.axis_index("col")
     rows = outer * inner
     my_outer, my_inner = lax.div(row, inner), lax.rem(row, inner)
+    part_loads = [
+        pltpu.make_async_copy(
+            part_hbm.at[block * inner + my_inner], part_ref.at[block], part_sem.at[block]
+        )
+        for block in range(outer)
+    ]
+    loads = [
+        pltpu.make_async_copy(source, target, load_sem.at[index])
+        for index, (source, target) in enumerate(
+            [(feat_hbm, feat_ref), (weight_hbm, weight_ref), (imp_hbm, imp_ref), (delta_hbm, delta_ref)]
+        )
+    ]
+    for load in part_loads + loads:
+        load.start()
     greet(
         [(peer, col) for peer in others(row, rows)] + [(row, peer) for peer in others(col, cols)]
     )
@@ -132,39 +251,65 @@
     def arrived(slot, sem):
         remote(slot, slot, sem, sem, (row, col)).wait_recv()
 
-    order = others(my_outer, outer) + [my_outer]
-    for block in order:
+    if outer == 4:
+        across = lax.rem(my_outer + 2, outer)
+        order = [across, mate_of(across), mate_of(my_outer), my_outer]
+    else:
+        order = others(my_outer, outer) + [my_outer]
+    halves = 2
+    height = part_ref.shape[1] // halves
+    steps = [(block, half) for block in order for half in range(halves)]
+
+    def strip(half):
+        return pl.ds(half * height, height)
+
+    def pair_sends(step):
+        block, half = steps[step]
+        return [
+            remote(
+                part_hbm.at[block * inner + peer, strip(half)],
+                pair_recv.at[my_inner, block, strip(half)],
+                pair_send_sem.at[peer, block, half],
+                pair_recv_sem.at[my_inner, block, half],
+                (my_outer * inner + peer, col),
+            )
+            for peer in others(my_inner, inner)
+        ]
+
+    for step in range(2):
+        for copy in pair_sends(step):
+            copy.start()
+    for load in part_loads + loads:
+        load.wait()
+    values = []
+    for step, (block, half) in enumerate(steps):
+        for copy in pair_sends(step):
+            copy.wait_send()
+        if step + 2 < len(steps):
+            for copy in pair_sends(step + 2):
+                copy.start()
+        value = part_ref[block, strip(half)].astype(jnp.float32)
         for peer in others(my_inner, inner):
+            arrived(pair_recv.at[peer, block, strip(half)], pair_recv_sem.at[peer, block, half])
+            value += pair_recv[peer, block, strip(half)].astype(jnp.float32)
+        if block is my_outer:
+            values.append(value)
+        else:
+            pair_sum[block, strip(half)] = value.astype(jnp.bfloat16)
             start(
                 remote(
-                    part_ref.at[block * inner + peer],
-                    pair_recv.at[my_inner, block],
-                    pair_send_sem.at[peer, block],
-                    pair_recv_sem.at[my_inner, block],
-                    (my_outer * inner + peer, col),
-                )
-            )
-    value = None
-    for block in order:
-        value = part_ref[block * inner + my_inner].astype(jnp.float32)
-        for peer in others(my_inner, inner):
-            arrived(pair_recv.at[peer, block], pair_recv_sem.at[peer, block])
-            value += pair_recv[peer, block].astype(jnp.float32)
-        if block is not my_outer:
-            pair_sum[block] = value.astype(jnp.bfloat16)
-            start(
-                remote(
-                    pair_sum.at[block],
-                    line_recv.at[my_outer],
-                    line_send_sem.at[block],
-                    line_recv_sem.at[my_outer],
+                    pair_sum.at[block, strip(half)],
+                    line_recv.at[my_outer, strip(half)],
+                    line_send_sem.at[block, half],
+                    line_recv_sem.at[my_outer, half],
                     (block * inner + my_inner, col),
                 )
             )
-    for peer in others(my_outer, outer):
-        arrived(line_recv.at[peer], line_recv_sem.at[peer])
-        value += line_recv[peer].astype(jnp.float32)
-    aggregate = value.astype(jnp.bfloat16)
+    for half in range(halves):
+        for peer in reversed(order[:-1]):
+            arrived(line_recv.at[peer, strip(half)], line_recv_sem.at[peer, half])
+            values[half] += line_recv[peer, strip(half)].astype(jnp.float32)
+    aggregate = jnp.concatenate(values, axis=0).astype(jnp.bfloat16)
 
     local_grad[...] = jnp.dot(
         aggregate, feat_ref[...], preferred_element_type=jnp.float32
@@ -188,6 +333,8 @@
         jnp.dot(weight_ref[...], aggregate, preferred_element_type=jnp.float32)
         .T.astype(jnp.bfloat16)
     )
+    grad_store = pltpu.make_async_copy(grad_ref, grad_hbm, store_sem.at[0])
+    grad_store.start()
     piece_sum = rows_of(local_grad, col)[...]
     for peer in others(col, cols):
         arrived(col_recv.at[peer], col_recv_sem.at[peer])
@@ -222,8 +369,12 @@
     for peer in others(col, cols):
         arrived(rows_of(whole_grad, peer), all_recv_sem.at[peer])
     imp_out_ref[...] = imp_ref[...] - whole_grad[...] * delta_ref[...]
+    imp_store = pltpu.make_async_copy(imp_out_ref, imp_out_hbm, store_sem.at[1])
+    imp_store.start()
     for copy in sends:
         copy.wait_send()
+    grad_store.wait()
+    imp_store.wait()
 
 
 def local(
@@ -248,15 +399,24 @@
     inner = 2 if rows % 2 == 0 else 1
     outer = rows // inner
     chunk = 16
-    params = functools.partial(pltpu.CompilerParams, vmem_limit_bytes=48 * 2**20)
+    params = functools.partial(pltpu.CompilerParams, vmem_limit_bytes=60 * 2**20)
     dma = pltpu.SemaphoreType.DMA
 
     masked = pl.pallas_call(
-        functools.partial(gather_kernel, cols),
+        functools.partial(gather_kernel, cols, 4),
         out_shape=jax.ShapeDtypeStruct((cols, own_width, block_nodes), jnp.bfloat16),
-        in_specs=[VMEM] * 2,
-        out_specs=VMEM,
-        scratch_shapes=[dma((cols,)), dma((cols,))],
+        in_specs=[HBM] * 2,
+        out_specs=HBM,
+        scratch_shapes=[
+            pltpu.VMEM((own_width, block_nodes), jnp.bfloat16),
+            pltpu.VMEM((own_width, block_nodes), jnp.int32),
+            pltpu.VMEM((own_width, block_nodes), jnp.bfloat16),
+            dma((2,)),
+            dma((1,)),
+            dma((cols, 4)),
+            dma((cols, 4)),
+            dma((cols, 4)),
+        ],
         compiler_params=params(collective_id=0, has_side_effects=True),
         name="gather_masked",
     )(out_grad.T, relu_mask.T)
@@ -264,19 +424,25 @@
     partial_value = pl.pallas_call(
         functools.partial(tiles_kernel, chunk),
         out_shape=jax.ShapeDtypeStruct((rows, width, nodes), jnp.bfloat16),
-        in_specs=[SMEM, SMEM, SMEM, VMEM, pl.BlockSpec(memory_space=pl.ANY)],
-        out_specs=VMEM,
+        in_specs=[HBM, HBM, SMEM, HBM, HBM],
+        out_specs=HBM,
         scratch_shapes=[
             pltpu.VMEM((slots, side, side), jnp.bfloat16),
             pltpu.VMEM((columns + 1, width, side), jnp.float32),
+            pltpu.SMEM((1, slots), jnp.int32),
+            pltpu.SMEM((1, slots), jnp.int32),
+            pltpu.VMEM((width, block_nodes), jnp.bfloat16),
+            pltpu.VMEM((rows, width, nodes), jnp.bfloat16),
             dma((slots // chunk,)),
+            dma((3,)),
+            dma((rows,)),
         ],
         compiler_params=params(),
         name="tile_products",
     )(
-        tile_row.reshape(slots),
-        tile_col.reshape(slots),
-        tile_count.reshape(1),
+        tile_row.reshape(1, slots),
+        tile_col.reshape(1, slots),
+        tile_count,
         masked.reshape(width, block_nodes),
         tile_vals.reshape(slots, side, side),
     )
@@ -288,9 +454,19 @@
             jax.ShapeDtypeStruct((nodes, depth), jnp.bfloat16),
             jax.ShapeDtypeStruct((depth, width), jnp.float32),
         ),
-        in_specs=[VMEM] * 5,
-        out_specs=(VMEM, VMEM),
+        in_specs=[HBM] * 5,
+        out_specs=(HBM, HBM),
         scratch_shapes=[
+            pltpu.VMEM((outer, width, nodes), jnp.bfloat16),
+            pltpu.VMEM((nodes, depth), jnp.bfloat16),
+            pltpu.VMEM((depth, width), jnp.bfloat16),
+            pltpu.VMEM((depth, width), jnp.float32),
+            pltpu.VMEM((depth, width), jnp.float32),
+            pltpu.VMEM((nodes, depth), jnp.bfloat16),
+            pltpu.VMEM((depth, width), jnp.float32),
+            dma((4,)),
+            dma((outer,)),
+            dma((2,)),
             pltpu.VMEM((inner, outer, width, nodes), jnp.bfloat16),
             pltpu.VMEM((outer, width, nodes), jnp.bfloat16),
             pltpu.VMEM((outer, width, nodes), jnp.bfloat16),
@@ -298,10 +474,10 @@
             pltpu.VMEM((cols, piece, width), jnp.float32),
             pltpu.VMEM((rows, piece, width), jnp.float32),
             pltpu.VMEM((depth, width), jnp.float32),
-            dma((inner, outer)),
-            dma((inner, outer)),
-            dma((outer,)),
-            dma((outer,)),
+            dma((inner, outer, 2)),
+            dma((inner, outer, 2)),
+            dma((outer, 2)),
+            dma((outer, 2)),
             dma((cols,)),
             dma((cols,)),
             dma((rows,)),

time: 54.5 us -> 54.5 us (level)
  local copies, waits for them, and re-layouts: 4.5 us -> 3.04 us
  Pallas kernels: 48.8 us -> 50.1 us
    pallas_call x1, Pallas kernels: 4.23 us -> 9.78 us  [local(): pl.pallas_call(functools.partial(tiles_kernel, chunk), out_shape=jax.Shap...]
    pallas_call x1, Pallas kernels: 35.3 us -> 31.1 us  [local(): pl.pallas_call(functools.partial(reduce_kernel, outer, inner, cols), out_...]
    unnamed x18 -> x2, local copies, waits for them, and re-layouts: 4.5 us -> 3.04 us
where the time goes in v2:
time: 54.5 us
  Pallas kernels  50.1 us (92%)
  local copies, waits for them, and re-layouts  3.04 us (6%)
  between operations  1.3 us (2%)
    pallas_call x1, Pallas kernels, local(): pl.pallas_call(functools.partial(reduce_kernel, outer, inner, cols), out_...  31.1 us
    pallas_call x1, Pallas kernels, local(): pl.pallas_call(functools.partial(tiles_kernel, chunk), out_shape=jax.Shap...  9.78 us
    pallas_call x1, Pallas kernels, local(): pl.pallas_call(functools.partial(gather_kernel, cols, 4), out_shape=jax.S...  9.27 us
    unnamed x2, local copies, waits for them, and re-layouts  3.04 us

profile of v2, /device:TPU:0, one launch (start us, length us, event | category | flops | bytes accessed | tf_op | source)
XLA Modules:
  0.0 54.5 jit_solution(14395234350150177061)
XLA Ops:
  1.3 9.3 %gather_masked.1 = bf16[4,32,2048]{2,1,0:T(8,128)(2,1)} custom-call(bf16[32,2048]{1,0:T(8,128)(2,1)} %bitcast.9, s32[32,2048]{1,0:T(8,128)} %bitcast.8), custom_call_target="tpu_custom_call" | custom-call | tf_op jit(solution)/shard_map/gather_masked/pallas_call | solution.py:405
  10.6 9.8 %tile_products.1.part_hbm = bf16[8,128,512]{2,1,0:T(8,128)(2,1)} custom-call(s32[1,256]{1,0:T(1,128)} %bitcast.10, s32[1,256]{1,0:T(1,128)} %bitcast.11, s32[1,1]{1,0:T(1,128)S(6)} %copy.14.count_ref, bf16[128,2048]{1,0:T(8,128)(2,1)} %bitcast.7, bf16[256,128,128]{2,1,0:T(8,128)(2,1)} %bitcast.6), custom_call_target="tpu_custom_call" | custom-call | tf_op jit(solution)/shard_map/tile_products/pallas_call | solution.py:424
  20.3 31.1 %reduce_and_update.1 = (bf16[512,128]{1,0:T(8,128)(2,1)}, f32[128,128]{1,0:T(8,128)}) custom-call(bf16[8,128,512]{2,1,0:T(8,128)(2,1)} %tile_products.1.part_hbm, bf16[512,128]{1,0:T(8,128)(2,1)} %feat_hbm.1, bf16[128,128]{1,0:T(8,128)(2,1)} %weight_hbm.1, f32[128,128]{1,0:T(8,128)} %imp_hbm.1, f32[128,128]{1,0:T(8,128)} %delta_hbm.1), custom_call_target="tpu_custom_call" | custom-call | tf_op jit(solution)/shard_map/reduce_and_update/pallas_call | solution.py:451
  51.4 1.6 %copy.15 = bf16[512,128]{1,0:T(8,128)(2,1)} copy(bf16[512,128]{1,0:T(8,128)(2,1)} %get-tuple-element.4) | data formatting | bytes 262144
  53.0 1.5 %copy.16 = f32[128,128]{1,0:T(8,128)} copy(f32[128,128]{1,0:T(8,128)} %get-tuple-element.5) | data formatting | bytes 131072

commit v3 on v1

v3 whole, which is shorter than its diff:
```python
import functools

import jax
import jax.numpy as jnp
from jax import lax
from jax.experimental import pallas as pl
from jax.experimental.pallas import tpu as pltpu
from jax.sharding import PartitionSpec as P

MESH = pl.DeviceIdType.MESH
SMEM = pl.BlockSpec(memory_space=pltpu.SMEM)
HBM = pl.BlockSpec(memory_space=pltpu.HBM)
PARTS = 4
HALVES = 2
CHUNK = 16


def remote(src, dst, send_sem, recv_sem, device):
    return pltpu.make_async_remote_copy(
        src_ref=src,
        dst_ref=dst,
        send_sem=send_sem,
        recv_sem=recv_sem,
        device_id=device,
        device_id_type=MESH,
    )


def greet(devices):
    barrier = pltpu.get_barrier_semaphore()
    for device in devices:
        pl.semaphore_signal(barrier, inc=1, device_id=device, device_id_type=MESH)
    pl.semaphore_wait(barrier, len(devices))


def others(me, count):
    return [lax.rem(me + step, count) for step in range(1, count)]


def mate_of(index):
    return index + 1 - 2 * lax.rem(index, 2)


def sort_tables(cols, rows, count, columns):
    slots = cols.shape[1]
    shape = (slots, slots)
    lane = lax.broadcasted_iota(jnp.int32, shape, 1)
    sublane = lax.broadcasted_iota(jnp.int32, shape, 0)
    diagonal = lane == sublane
    here = jnp.broadcast_to(cols, shape)
    key = jnp.where(lane < count, here, columns)

    def upright(value):
        return jnp.sum(jnp.where(diagonal, value, 0), axis=1, keepdims=True)

    mine = upright(key)
    row = upright(jnp.broadcast_to(rows, shape))
    earlier = (key == mine) & (lane < sublane)
    rank = jnp.sum(jnp.where((key < mine) | earlier, 1, 0), axis=1, keepdims=True)
    keep = jnp.max(jnp.where(earlier, 1, 0), axis=1, keepdims=True)
    placed = rank == lane

    def in_order(value):
        return jnp.sum(jnp.where(placed, value, 0), axis=0, keepdims=True)

    first = jnp.sum(jnp.where(mine < lane, 1, 0), axis=0, keepdims=True)
    last = jnp.sum(jnp.where(mine <= lane, 1, 0), axis=0, keepdims=True)
    return in_order(sublane), in_order(row), in_order(keep), first, last


def layer_kernel(
    outer,
    inner,
    cols,
    rows_hbm,
    cols_hbm,
    count_ref,
    grad_hbm,
    mask_hbm,
    vals_hbm,
    feat_hbm,
    weight_hbm,
    node_out_hbm,
    weight_out_hbm,
    grad_ref,
    mask_ref,
    masked_ref,
    held,
    tile_rows_ref,
    tile_cols_ref,
    table_ref,
    table,
    sums,
    part_ref,
    feat_ref,
    weight_ref,
    node_out_ref,
    pair_recv,
    pair_sum,
    line_recv,
    local_grad,
    col_recv,
    row_recv,
    whole_grad,
    load_sem,
    tile_sem,
    table_sem,
    store_sem,
    send_sem,
    pass_sem,
    recv_sem,
    pair_send_sem,
    pair_recv_sem,
    line_send_sem,
    line_recv_sem,
    col_send_sem,
    col_recv_sem,
    row_send_sem,
    row_recv_sem,
    all_send_sem,
    all_recv_sem,
):
    row, col = lax.axis_index("row"), lax.axis_index("col")
    rows = outer * inner
    my_outer, my_inner = lax.div(row, inner), lax.rem(row, inner)
    slots, side = held.shape[0], held.shape[-1]
    width, nodes = part_ref.shape[1:]
    per_block = nodes // side
    columns = rows * per_block
    sends = []

    def start(copy):
        copy.start()
        sends.append(copy)

    def arrived(slot, sem):
        remote(slot, slot, sem, sem, (row, mate_of(col))).wait_recv()

    loads = [
        pltpu.make_async_copy(source, target, load_sem.at[index])
        for index, (source, target) in enumerate(
            [
                (grad_hbm, grad_ref),
                (mask_hbm, mask_ref),
                (rows_hbm, tile_rows_ref),
                (cols_hbm, tile_cols_ref),
                (feat_hbm, feat_ref),
                (weight_hbm, weight_ref),
            ]
        )
    ]
    for load in loads:
        load.start()
    tile_loads = []
    for index in range(slots // CHUNK):
        piece = pl.ds(index * CHUNK, CHUNK)
        load = pltpu.make_async_copy(vals_hbm.at[piece], held.at[piece], tile_sem.at[index])
        load.start()
        tile_loads.append(load)
    greet(
        [(row, peer) for peer in others(col, cols)] + [(peer, col) for peer in others(row, rows)]
    )

    loads[0].wait()
    loads[1].wait()
    mate = mate_of(col)
    far = [lax.rem(col + 2 * step, cols) for step in range(1, cols // 2)]
    row_tiles = masked_ref.shape[0]
    size = row_tiles // PARTS
    own_width = grad_ref.shape[0]

    def masked_piece(block, part):
        lines = pl.ds(pl.multiple_of(block * own_width, own_width), own_width)
        return masked_ref.at[part * size : (part + 1) * size, lines]

    def send_masked(block, part, sems, peer):
        ref = masked_piece(block, part)
        start(remote(ref, ref, sems.at[peer, part], recv_sem.at[block, part], (row, peer)))

    def masked_arrived(block, part):
        arrived(masked_piece(block, part), recv_sem.at[block, part])

    for part in range(PARTS):
        for tile in range(part * size, (part + 1) * size):
            lanes = slice(tile * side, (tile + 1) * side)
            lines = pl.ds(pl.multiple_of(col * own_width, own_width), own_width)
            masked_ref[tile, lines, :] = (
                grad_ref[:, lanes].astype(jnp.float32) * mask_ref[:, lanes].astype(jnp.float32)
            ).astype(jnp.bfloat16)
        for peer in far:
            send_masked(col, part, send_sem, peer)
    for part in range(PARTS):
        send_masked(col, part, send_sem, mate)
    loads[2].wait()
    loads[3].wait()
    for index, line in enumerate(
        sort_tables(tile_cols_ref[...], tile_rows_ref[...], count_ref[0, 0], columns)
    ):
        table_ref[index : index + 1, :] = line
    to_scalars = pltpu.make_async_copy(table_ref, table, table_sem.at[0])
    to_scalars.start()
    for part in range(PARTS):
        for peer in far:
            masked_arrived(peer, part)
            send_masked(peer, part, pass_sem, mate)
    to_scalars.wait()
    for load in tile_loads + loads[4:]:
        load.wait()
    for part in range(PARTS):
        masked_arrived(mate, part)
        for peer in far:
            masked_arrived(mate_of(peer), part)

    def chunk_step(index, running):
        for step in range(CHUNK):
            place = index * CHUNK + step
            product = jnp.dot(
                masked_ref[table[1, place]],
                held[table[0, place]],
                preferred_element_type=jnp.float32,
            )
            running = running * table[2, place].astype(jnp.float32) + product
            sums[place] = running.astype(jnp.bfloat16)
        return running

    lax.fori_loop(0, slots // CHUNK, chunk_step, jnp.zeros((width, side), jnp.float32))

    def pack(block):
        for part in range(per_block):
            column = block * per_block + part
            begin, end = table[3, column], table[4, column]
            used = jnp.minimum(end - begin, 1).astype(jnp.float32)
            value = sums[jnp.maximum(end - 1, 0)].astype(jnp.float32) * used
            part_ref[block, :, part * side : (part + 1) * side] = value.astype(jnp.bfloat16)

    if outer == 4:
        across = lax.rem(my_outer + 2, outer)
        order = [across, mate_of(across), mate_of(my_outer), my_outer]
    else:
        order = others(my_outer, outer) + [my_outer]
    height = width // HALVES
    steps = [(block, half) for block in order for half in range(HALVES)]

    def strip(half):
        return pl.ds(half * height, height)

    def pair_sends(step):
        block, half = steps[step]
        return [
            remote(
                part_ref.at[block * inner + peer, strip(half)],
                pair_recv.at[my_inner, block, strip(half)],
                pair_send_sem.at[peer, block, half],
                pair_recv_sem.at[my_inner, block, half],
                (my_outer * inner + peer, col),
            )
            for peer in others(my_inner, inner)
        ]

    for index, block in enumerate(order):
        for peer in others(my_inner, inner):
            pack(block * inner + peer)
        if index == 0:
            for step in range(2):
                for copy in pair_sends(step):
                    copy.start()
    for block in order:
        pack(block * inner + my_inner)
    values = []
    for step, (block, half) in enumerate(steps):
        for copy in pair_sends(step):
            copy.wait_send()
        if step + 2 < len(steps):
            for copy in pair_sends(step + 2):
                copy.start()
        value = part_ref[block * inner + my_inner, strip(half)].astype(jnp.float32)
        for peer in others(my_inner, inner):
            arrived(pair_recv.at[peer, block, strip(half)], pair_recv_sem.at[peer, block, half])
            value += pair_recv[peer, block, strip(half)].astype(jnp.float32)
        if block is my_outer:
            values.append(value)
        else:
            pair_sum[block, strip(half)] = value.astype(jnp.bfloat16)
            start(
                remote(
                    pair_sum.at[block, strip(half)],
                    line_recv.at[my_outer, strip(half)],
                    line_send_sem.at[block, half],
                    line_recv_sem.at[my_outer, half],
                    (block * inner + my_inner, col),
                )
            )
    for half in range(HALVES):
        for peer in reversed(order[:-1]):
            arrived(line_recv.at[peer, strip(half)], line_recv_sem.at[peer, half])
            values[half] += line_recv[peer, strip(half)].astype(jnp.float32)
    aggregate = jnp.concatenate(values, axis=0).astype(jnp.bfloat16)

    local_grad[...] = jnp.dot(
        aggregate, feat_ref[...], preferred_element_type=jnp.float32
    ).T
    piece = local_grad.shape[0] // cols

    def rows_of(ref, index):
        return ref.at[pl.ds(pl.multiple_of(index * piece, piece), piece)]

    for peer in others(col, cols):
        start(
            remote(
                rows_of(local_grad, peer),
                col_recv.at[col],
                col_send_sem.at[peer],
                col_recv_sem.at[col],
                (row, peer),
            )
        )
    node_out_ref[...] = (
        jnp.dot(weight_ref[...], aggregate, preferred_element_type=jnp.float32)
        .T.astype(jnp.bfloat16)
    )
    node_store = pltpu.make_async_copy(node_out_ref, node_out_hbm, store_sem.at[0])
    node_store.start()
    piece_sum = rows_of(local_grad, col)[...]
    for peer in others(col, cols):
        arrived(col_recv.at[peer], col_recv_sem.at[peer])
        piece_sum += col_recv[peer]
    row_recv[row] = piece_sum
    for peer in others(row, rows):
        start(
            remote(
                row_recv.at[row],
                row_recv.at[row],
                row_send_sem.at[peer],
                row_recv_sem.at[row],
                (peer, col),
            )
        )
    for peer in others(row, rows):
        arrived(row_recv.at[peer], row_recv_sem.at[peer])
    piece_sum = row_recv[0]
    for index in range(1, rows):
        piece_sum += row_recv[index]
    rows_of(whole_grad, col)[...] = piece_sum
    for peer in others(col, cols):
        start(
            remote(
                rows_of(whole_grad, col),
                rows_of(whole_grad, col),
                all_send_sem.at[peer],
                all_recv_sem.at[col],
                (row, peer),
            )
        )
    for peer in others(col, cols):
        arrived(rows_of(whole_grad, peer), all_recv_sem.at[peer])
    weight_store = pltpu.make_async_copy(whole_grad, weight_out_hbm, store_sem.at[1])
    weight_store.start()
    for copy in sends:
        copy.wait_send()
    node_store.wait()
    weight_store.wait()


def finish_kernel(
    node_hbm, grad_hbm, imp_hbm, delta_hbm, node_out, imp_out, node_ref, grad_ref, imp_ref, delta_ref, sems
):
    loads = [
        pltpu.make_async_copy(source, target, sems.at[index])
        for index, (source, target) in enumerate(
            [(node_hbm, node_ref), (grad_hbm, grad_ref), (imp_hbm, imp_ref), (delta_hbm, delta_ref)]
        )
    ]
    for load in loads:
        load.start()
    loads[0].wait()
    node_store = pltpu.make_async_copy(node_ref, node_out, sems.at[4])
    node_store.start()
    for load in loads[1:]:
        load.wait()
    imp_ref[...] = imp_ref[...] - grad_ref[...] * delta_ref[...]
    imp_store = pltpu.make_async_copy(imp_ref, imp_out, sems.at[5])
    imp_store.start()
    node_store.wait()
    imp_store.wait()


def local(
    rows,
    cols,
    tile_vals,
    tile_row,
    tile_col,
    tile_count,
    out_grad,
    relu_mask,
    features,
    weight,
    importance,
    weight_delta,
):
    slots, side = tile_vals.shape[2], tile_vals.shape[-1]
    nodes, depth = features.shape
    block_nodes, own_width = out_grad.shape
    width = own_width * cols
    inner = 2 if rows % 2 == 0 else 1
    outer = rows // inner
    params = functools.partial(pltpu.CompilerParams, vmem_limit_bytes=60 * 2**20)
    dma = pltpu.SemaphoreType.DMA
    piece = depth // cols
    bf16 = jnp.bfloat16
    f32 = jnp.float32
    i32 = jnp.int32

    node_grad, weight_grad = pl.pallas_call(
        functools.partial(layer_kernel, outer, inner, cols),
        out_shape=(
            jax.ShapeDtypeStruct((nodes, depth), bf16),
            jax.ShapeDtypeStruct((depth, width), f32),
        ),
        in_specs=[HBM, HBM, SMEM] + [HBM] * 5,
        out_specs=(HBM, HBM),
        scratch_shapes=[
            pltpu.VMEM((own_width, block_nodes), bf16),
            pltpu.VMEM((own_width, block_nodes), i32),
            pltpu.VMEM((block_nodes // side, width, side), bf16),
            pltpu.VMEM((slots, side, side), bf16),
            pltpu.VMEM((1, slots), i32),
            pltpu.VMEM((1, slots), i32),
            pltpu.VMEM((8, slots), i32),
            pltpu.SMEM((8, slots), i32),
            pltpu.VMEM((slots, width, side), bf16),
            pltpu.VMEM((rows, width, nodes), bf16),
            pltpu.VMEM((nodes, depth), bf16),
            pltpu.VMEM((depth, width), bf16),
            pltpu.VMEM((nodes, depth), bf16),
            pltpu.VMEM((inner, outer, width, nodes), bf16),
            pltpu.VMEM((outer, width, nodes), bf16),
            pltpu.VMEM((outer, width, nodes), bf16),
            pltpu.VMEM((depth, width), f32),
            pltpu.VMEM((cols, piece, width), f32),
            pltpu.VMEM((rows, piece, width), f32),
            pltpu.VMEM((depth, width), f32),
            dma((6,)),
            dma((slots // CHUNK,)),
            dma((1,)),
            dma((2,)),
            dma((cols, PARTS)),
            dma((cols, PARTS)),
            dma((cols, PARTS)),
            dma((inner, outer, HALVES)),
            dma((inner, outer, HALVES)),
            dma((outer, HALVES)),
            dma((outer, HALVES)),
            dma((cols,)),
            dma((cols,)),
            dma((rows,)),
            dma((rows,)),
            dma((cols,)),
            dma((cols,)),
        ],
        compiler_params=params(collective_id=0, has_side_effects=True),
        name="layer_backward",
    )(
        tile_row.reshape(1, slots),
        tile_col.reshape(1, slots),
        tile_count,
        out_grad.T,
        relu_mask.T,
        tile_vals.reshape(slots, side, side),
        features,
        weight,
    )

    return pl.pallas_call(
        finish_kernel,
        out_shape=(
            jax.ShapeDtypeStruct((nodes, depth), bf16),
            jax.ShapeDtypeStruct((depth, width), f32),
        ),
        in_specs=[HBM] * 4,
        out_specs=(HBM, HBM),
        scratch_shapes=[
            pltpu.VMEM((nodes, depth), bf16),
            pltpu.VMEM((depth, width), f32),
            pltpu.VMEM((depth, width), f32),
            pltpu.VMEM((depth, width), f32),
            dma((6,)),
        ],
        compiler_params=params(),
        name="finish",
    )(node_grad, weight_grad, importance, weight_delta)


def solution(mesh):
    return jax.shard_map(
        functools.partial(local, mesh.shape["row"], mesh.shape["col"]),
        mesh=mesh,
        in_specs=(
            P("row", "col", None, None, None),
            P("row", "col", None),
            P("row", "col", None),
            P("row", "col"),
            P("row", "col"),
            P("row", "col"),
            P(("row", "col"), None),
            P(),
            P(),
            P(),
        ),
        out_specs=(P(("row", "col"), None), P()),
        check_vma=False,
    )
```

time: 54.5 us -> 48.1 us (0.88)
  local copies, waits for them, and re-layouts: 4.5 us -> 0 us
  Pallas kernels: 48.8 us -> 46.7 us
    unnamed x18 -> x0, local copies, waits for them, and re-layouts: 4.5 us -> none
    pallas_call x3 -> x2, Pallas kernels: 48.8 us -> 46.7 us  [the longest x1 45 us: local(): pl.pallas_call(functools.partial(layer_kernel, outer, inner, cols), out_s...]
where the time goes in v3:
time: 48.1 us; the launch traced here: 48 us
  Pallas kernels  46.7 us (97%)
  between operations  1.29 us (3%)
    pallas_call x1, Pallas kernels, local(): pl.pallas_call(functools.partial(layer_kernel, outer, inner, cols), out_s...  45 us
    pallas_call x1, Pallas kernels, local(): pl.pallas_call(finish_kernel, out_shape=(jax.ShapeDtypeStruct((nodes, dep...  1.66 us

profile of v3, /device:TPU:0, one launch (start us, length us, event | category | flops | bytes accessed | tf_op | source)
XLA Modules:
  0.0 48.0 jit_solution(15294171023037237988)
XLA Ops:
  1.3 45.0 %layer_backward.1 = (bf16[512,128]{1,0:T(8,128)(2,1)}, f32[128,128]{1,0:T(8,128)}) custom-call(s32[1,256]{1,0:T(1,128)} %bitcast.8, s32[1,256]{1,0:T(1,128)} %bitcast.9, s32[1,1]{1,0:T(1,128)S(6)} %copy.12.count_ref, bf16[32,2048]{1,0:T(8,128)(2,1)} %bitcast.7, s32[32,2048]{1,0:T(8,128)} %bitcast.6, bf16[256,128,128]{2,1,0:T(8,128)(2,1)} %bitcast.5, ...), custom_call_target="tpu_custom_call" | custom-call | tf_op jit(solution)/shard_map/layer_backward/pallas_call | solution.py:414
  46.3 1.7 %finish.1 = (bf16[512,128]{1,0:T(8,128)(2,1)}, f32[128,128]{1,0:T(8,128)}) custom-call(bf16[512,128]{1,0:T(8,128)(2,1)} %get-tuple-element.4.node_hbm, f32[128,128]{1,0:T(8,128)} %get-tuple-element.5.grad_hbm, f32[128,128]{1,0:T(8,128)} %imp_hbm.1, f32[128,128]{1,0:T(8,128)} %delta_hbm.1), custom_call_target="tpu_custom_call" | custom-call | tf_op jit(solution)/shard_map/finish/pallas_call | solution.py:474

commit v4 on v3

--- a/solution.py
+++ b/solution.py
@@ -119,6 +119,8 @@
     row_recv_sem,
     all_send_sem,
     all_recv_sem,
+    feat_send_sem,
+    feat_recv_sem,
 ):
     row, col = lax.axis_index("row"), lax.axis_index("col")
     rows = outer * inner
@@ -136,6 +138,12 @@
     def arrived(slot, sem):
         remote(slot, slot, sem, sem, (row, mate_of(col))).wait_recv()
 
+    if outer == 4:
+        across = lax.rem(my_outer + 2, outer)
+        order = [across, mate_of(across), mate_of(my_outer), my_outer]
+    else:
+        order = others(my_outer, outer) + [my_outer]
+
     loads = [
         pltpu.make_async_copy(source, target, load_sem.at[index])
         for index, (source, target) in enumerate(
@@ -144,7 +152,7 @@
                 (mask_hbm, mask_ref),
                 (rows_hbm, tile_rows_ref),
                 (cols_hbm, tile_cols_ref),
-                (feat_hbm, feat_ref),
+                (feat_hbm, feat_ref.at[my_outer]),
                 (weight_hbm, weight_ref),
             ]
         )
@@ -191,6 +199,16 @@
             send_masked(col, part, send_sem, peer)
     for part in range(PARTS):
         send_masked(col, part, send_sem, mate)
+    for peer in order[:-1]:
+        start(
+            remote(
+                feat_hbm,
+                feat_ref.at[my_outer],
+                feat_send_sem.at[peer],
+                feat_recv_sem.at[my_outer],
+                (peer * inner + my_inner, col),
+            )
+        )
     loads[2].wait()
     loads[3].wait()
     for index, line in enumerate(
@@ -233,11 +251,6 @@
             value = sums[jnp.maximum(end - 1, 0)].astype(jnp.float32) * used
             part_ref[block, :, part * side : (part + 1) * side] = value.astype(jnp.bfloat16)
 
-    if outer == 4:
-        across = lax.rem(my_outer + 2, outer)
-        order = [across, mate_of(across), mate_of(my_outer), my_outer]
-    else:
-        order = others(my_outer, outer) + [my_outer]
     height = width // HALVES
     steps = [(block, half) for block in order for half in range(HALVES)]
 
@@ -267,6 +280,7 @@
     for block in order:
         pack(block * inner + my_inner)
     values = []
+    grads = [0.0] * HALVES
     for step, (block, half) in enumerate(steps):
         for copy in pair_sends(step):
             copy.wait_send()
@@ -277,10 +291,11 @@
         for peer in others(my_inner, inner):
             arrived(pair_recv.at[peer, block, strip(half)], pair_recv_sem.at[peer, block, half])
             value += pair_recv[peer, block, strip(half)].astype(jnp.float32)
+        rounded = value.astype(jnp.bfloat16)
         if block is my_outer:
             values.append(value)
         else:
-            pair_sum[block, strip(half)] = value.astype(jnp.bfloat16)
+            pair_sum[block, strip(half)] = rounded
             start(
                 remote(
                     pair_sum.at[block, strip(half)],
@@ -290,15 +305,10 @@
                     (block * inner + my_inner, col),
                 )
             )
-    for half in range(HALVES):
-        for peer in reversed(order[:-1]):
-            arrived(line_recv.at[peer, strip(half)], line_recv_sem.at[peer, half])
-            values[half] += line_recv[peer, strip(half)].astype(jnp.float32)
-    aggregate = jnp.concatenate(values, axis=0).astype(jnp.bfloat16)
-
-    local_grad[...] = jnp.dot(
-        aggregate, feat_ref[...], preferred_element_type=jnp.float32
-    ).T
+            if half == 0:
+                arrived(feat_ref.at[block], feat_recv_sem.at[block])
+        grads[half] += jnp.dot(rounded, feat_ref[block], preferred_element_type=jnp.float32)
+    local_grad[...] = jnp.concatenate(grads, axis=0).T
     piece = local_grad.shape[0] // cols
 
     def rows_of(ref, index):
@@ -314,17 +324,11 @@
                 (row, peer),
             )
         )
-    node_out_ref[...] = (
-        jnp.dot(weight_ref[...], aggregate, preferred_element_type=jnp.float32)
-        .T.astype(jnp.bfloat16)
-    )
-    node_store = pltpu.make_async_copy(node_out_ref, node_out_hbm, store_sem.at[0])
-    node_store.start()
     piece_sum = rows_of(local_grad, col)[...]
     for peer in others(col, cols):
         arrived(col_recv.at[peer], col_recv_sem.at[peer])
         piece_sum += col_recv[peer]
-    row_recv[row] = piece_sum
+    row_recv[row] = piece_sum.astype(jnp.bfloat16)
     for peer in others(row, rows):
         start(
             remote(
@@ -335,11 +339,22 @@
                 (peer, col),
             )
         )
+    for half in range(HALVES):
+        for peer in reversed(order[:-1]):
+            arrived(line_recv.at[peer, strip(half)], line_recv_sem.at[peer, half])
+            values[half] += line_recv[peer, strip(half)].astype(jnp.float32)
+    aggregate = jnp.concatenate(values, axis=0).astype(jnp.bfloat16)
+    node_out_ref[...] = (
+        jnp.dot(weight_ref[...], aggregate, preferred_element_type=jnp.float32)
+        .T.astype(jnp.bfloat16)
+    )
+    node_store = pltpu.make_async_copy(node_out_ref, node_out_hbm, store_sem.at[0])
+    node_store.start()
     for peer in others(row, rows):
         arrived(row_recv.at[peer], row_recv_sem.at[peer])
-    piece_sum = row_recv[0]
+    piece_sum = row_recv[0].astype(jnp.float32)
     for index in range(1, rows):
-        piece_sum += row_recv[index]
+        piece_sum += row_recv[index].astype(jnp.float32)
     rows_of(whole_grad, col)[...] = piece_sum
     for peer in others(col, cols):
         start(
@@ -430,7 +445,7 @@
             pltpu.SMEM((8, slots), i32),
             pltpu.VMEM((slots, width, side), bf16),
             pltpu.VMEM((rows, width, nodes), bf16),
-            pltpu.VMEM((nodes, depth), bf16),
+            pltpu.VMEM((outer, nodes, depth), bf16),
             pltpu.VMEM((depth, width), bf16),
             pltpu.VMEM((nodes, depth), bf16),
             pltpu.VMEM((inner, outer, width, nodes), bf16),
@@ -438,7 +453,7 @@
             pltpu.VMEM((outer, width, nodes), bf16),
             pltpu.VMEM((depth, width), f32),
             pltpu.VMEM((cols, piece, width), f32),
-            pltpu.VMEM((rows, piece, width), f32),
+            pltpu.VMEM((rows, piece, width), bf16),
             pltpu.VMEM((depth, width), f32),
             dma((6,)),
             dma((slots // CHUNK,)),
@@ -457,6 +472,8 @@
             dma((rows,)),
             dma((cols,)),
             dma((cols,)),
+            dma((outer,)),
+            dma((outer,)),
         ],
         compiler_params=params(collective_id=0, has_side_effects=True),
         name="layer_backward",

time: 48.1 us -> 44.2 us (0.919)
  Pallas kernels: 46.7 us -> 42.7 us
    pallas_call x1, Pallas kernels: 45 us -> 41.1 us  [local(): pl.pallas_call(functools.partial(layer_kernel, outer, inner, cols), out_s...]
where the time goes in v4:
time: 44.2 us; the launch traced here: 44 us
  Pallas kernels  42.7 us (97%)
  between operations  1.29 us (3%)
    pallas_call x1, Pallas kernels, local(): pl.pallas_call(functools.partial(layer_kernel, outer, inner, cols), out_s...  41.1 us
    pallas_call x1, Pallas kernels, local(): pl.pallas_call(finish_kernel, out_shape=(jax.ShapeDtypeStruct((nodes, dep...  1.66 us

profile of v4, /device:TPU:0, one launch (start us, length us, event | category | flops | bytes accessed | tf_op | source)
XLA Modules:
  0.0 44.0 jit_solution(4273562936988502795)
XLA Ops:
  1.3 41.1 %layer_backward.1 = (bf16[512,128]{1,0:T(8,128)(2,1)}, f32[128,128]{1,0:T(8,128)}) custom-call(s32[1,256]{1,0:T(1,128)} %bitcast.8, s32[1,256]{1,0:T(1,128)} %bitcast.9, s32[1,1]{1,0:T(1,128)S(6)} %copy.12.count_ref, bf16[32,2048]{1,0:T(8,128)(2,1)} %bitcast.7, s32[32,2048]{1,0:T(8,128)} %bitcast.6, bf16[256,128,128]{2,1,0:T(8,128)(2,1)} %bitcast.5, ...), custom_call_target="tpu_custom_call" | custom-call | tf_op jit(solution)/shard_map/layer_backward/pallas_call | solution.py:429
  42.4 1.7 %finish.1 = (bf16[512,128]{1,0:T(8,128)(2,1)}, f32[128,128]{1,0:T(8,128)}) custom-call(bf16[512,128]{1,0:T(8,128)(2,1)} %get-tuple-element.4.node_hbm, f32[128,128]{1,0:T(8,128)} %get-tuple-element.5.grad_hbm, f32[128,128]{1,0:T(8,128)} %imp_hbm.1, f32[128,128]{1,0:T(8,128)} %delta_hbm.1), custom_call_target="tpu_custom_call" | custom-call | tf_op jit(solution)/shard_map/finish/pallas_call | solution.py:491

commit v5 on v4

--- a/solution.py
+++ b/solution.py
@@ -11,7 +11,6 @@
 SMEM = pl.BlockSpec(memory_space=pltpu.SMEM)
 HBM = pl.BlockSpec(memory_space=pltpu.HBM)
 PARTS = 4
-HALVES = 2
 CHUNK = 16
 
 
@@ -24,13 +23,6 @@
         device_id=device,
         device_id_type=MESH,
     )
-
-
-def greet(devices):
-    barrier = pltpu.get_barrier_semaphore()
-    for device in devices:
-        pl.semaphore_signal(barrier, inc=1, device_id=device, device_id_type=MESH)
-    pl.semaphore_wait(barrier, len(devices))
 
 
 def others(me, count):
@@ -84,13 +76,15 @@
     weight_out_hbm,
     grad_ref,
     mask_ref,
-    masked_ref,
+    near_ref,
+    far_ref,
     held,
     tile_rows_ref,
     tile_cols_ref,
     table_ref,
     table,
-    sums,
+    near_sums,
+    far_sums,
     part_ref,
     feat_ref,
     weight_ref,
@@ -102,6 +96,7 @@
     col_recv,
     row_recv,
     whole_grad,
+    aggregate,
     load_sem,
     tile_sem,
     table_sem,
@@ -165,40 +160,63 @@
         load = pltpu.make_async_copy(vals_hbm.at[piece], held.at[piece], tile_sem.at[index])
         load.start()
         tile_loads.append(load)
-    greet(
-        [(row, peer) for peer in others(col, cols)] + [(peer, col) for peer in others(row, rows)]
-    )
+    partners = [(row, peer) for peer in others(col, cols)] + [
+        (peer, col) for peer in others(row, rows)
+    ]
+    barrier = pltpu.get_barrier_semaphore()
+    for partner in partners:
+        pl.semaphore_signal(barrier, inc=1, device_id=partner, device_id_type=MESH)
+
+    loads[2].wait()
+    loads[3].wait()
+    for index, line in enumerate(
+        sort_tables(tile_cols_ref[...], tile_rows_ref[...], count_ref[0, 0], columns)
+    ):
+        table_ref[index : index + 1, :] = line
+    to_scalars = pltpu.make_async_copy(table_ref, table, table_sem.at[0])
+    to_scalars.start()
 
     loads[0].wait()
     loads[1].wait()
     mate = mate_of(col)
+    first = col - lax.rem(col, 2)
     far = [lax.rem(col + 2 * step, cols) for step in range(1, cols // 2)]
-    row_tiles = masked_ref.shape[0]
+    row_tiles = near_ref.shape[0]
     size = row_tiles // PARTS
     own_width = grad_ref.shape[0]
 
-    def masked_piece(block, part):
-        lines = pl.ds(pl.multiple_of(block * own_width, own_width), own_width)
-        return masked_ref.at[part * size : (part + 1) * size, lines]
-
-    def send_masked(block, part, sems, peer):
-        ref = masked_piece(block, part)
-        start(remote(ref, ref, sems.at[peer, part], recv_sem.at[block, part], (row, peer)))
-
-    def masked_arrived(block, part):
-        arrived(masked_piece(block, part), recv_sem.at[block, part])
-
+    def tiles_of(part):
+        return pl.ds(part * size, size)
+
+    def lines_of(position):
+        return pl.ds(pl.multiple_of(position * own_width, own_width), own_width)
+
+    def near_piece(block, part):
+        return near_ref.at[tiles_of(part), lines_of(lax.rem(block, 2))]
+
+    def far_piece(block, part, device):
+        position = lax.rem(block - (device - lax.rem(device, 2)) + cols, cols) - 2
+        return far_ref.at[tiles_of(part), lines_of(position)]
+
+    for tile in range(row_tiles):
+        lanes = slice(tile * side, (tile + 1) * side)
+        near_ref[tile, lines_of(lax.rem(col, 2)), :] = (
+            grad_ref[:, lanes].astype(jnp.float32) * mask_ref[:, lanes].astype(jnp.float32)
+        ).astype(jnp.bfloat16)
+    pl.semaphore_wait(barrier, len(partners))
     for part in range(PARTS):
-        for tile in range(part * size, (part + 1) * size):
-            lanes = slice(tile * side, (tile + 1) * side)
-            lines = pl.ds(pl.multiple_of(col * own_width, own_width), own_width)
-            masked_ref[tile, lines, :] = (
-                grad_ref[:, lanes].astype(jnp.float32) * mask_ref[:, lanes].astype(jnp.float32)
-            ).astype(jnp.bfloat16)
         for peer in far:
-            send_masked(col, part, send_sem, peer)
-    for part in range(PARTS):
-        send_masked(col, part, send_sem, mate)
+            start(
+                remote(
+                    near_piece(col, part),
+                    far_piece(col, part, peer),
+                    send_sem.at[peer, part],
+                    recv_sem.at[col, part],
+                    (row, peer),
+                )
+            )
+        ref = near_piece(col, part)
+        start(remote(ref, ref, send_sem.at[mate, part], recv_sem.at[col, part], (row, mate)))
     for peer in order[:-1]:
         start(
             remote(
@@ -209,53 +227,53 @@
                 (peer * inner + my_inner, col),
             )
         )
-    loads[2].wait()
-    loads[3].wait()
-    for index, line in enumerate(
-        sort_tables(tile_cols_ref[...], tile_rows_ref[...], count_ref[0, 0], columns)
-    ):
-        table_ref[index : index + 1, :] = line
-    to_scalars = pltpu.make_async_copy(table_ref, table, table_sem.at[0])
-    to_scalars.start()
-    for part in range(PARTS):
-        for peer in far:
-            masked_arrived(peer, part)
-            send_masked(peer, part, pass_sem, mate)
-    to_scalars.wait()
-    for load in tile_loads + loads[4:]:
-        load.wait()
-    for part in range(PARTS):
-        masked_arrived(mate, part)
-        for peer in far:
-            masked_arrived(mate_of(peer), part)
-
-    def chunk_step(index, running):
-        for step in range(CHUNK):
-            place = index * CHUNK + step
-            product = jnp.dot(
-                masked_ref[table[1, place]],
-                held[table[0, place]],
-                preferred_element_type=jnp.float32,
-            )
-            running = running * table[2, place].astype(jnp.float32) + product
-            sums[place] = running.astype(jnp.bfloat16)
-        return running
-
-    lax.fori_loop(0, slots // CHUNK, chunk_step, jnp.zeros((width, side), jnp.float32))
-
-    def pack(block):
+
+    def products(masked_ref, sums, begin, end, running):
+        def chunk_step(index, running):
+            for step in range(CHUNK):
+                place = index * CHUNK + step
+                product = jnp.dot(
+                    masked_ref[table[1, place]],
+                    held[table[0, place]],
+                    preferred_element_type=jnp.float32,
+                )
+                running = running * table[2, place].astype(jnp.float32) + product
+                sums[place] = running.astype(jnp.bfloat16)
+            return running
+
+        return lax.fori_loop(begin, end, chunk_step, running)
+
+    near = near_ref.shape[1]
+    strips = [pl.ds(0, near), pl.ds(near, width - near)]
+
+    def pack(sums, strip, block):
         for part in range(per_block):
             column = block * per_block + part
             begin, end = table[3, column], table[4, column]
             used = jnp.minimum(end - begin, 1).astype(jnp.float32)
             value = sums[jnp.maximum(end - 1, 0)].astype(jnp.float32) * used
-            part_ref[block, :, part * side : (part + 1) * side] = value.astype(jnp.bfloat16)
-
-    height = width // HALVES
-    steps = [(block, half) for block in order for half in range(HALVES)]
+            part_ref[block, strip, part * side : (part + 1) * side] = value.astype(jnp.bfloat16)
+
+    to_scalars.wait()
+    for load in tile_loads + loads[4:]:
+        load.wait()
+    for part in range(PARTS):
+        arrived(near_piece(mate, part), recv_sem.at[mate, part])
+    chunks = slots // CHUNK
+    pause = chunks * 3 // 4
+    zeros = jnp.zeros((near, side), jnp.float32)
+    running = products(near_ref, near_sums, 0, pause, zeros)
+    for part in range(PARTS):
+        for peer in far:
+            ref = far_piece(peer, part, col)
+            arrived(ref, recv_sem.at[peer, part])
+            start(remote(ref, ref, pass_sem.at[peer, part], recv_sem.at[peer, part], (row, mate)))
+    products(near_ref, near_sums, pause, chunks, running)
+
+    steps = [(block, half) for half in range(2) for block in order]
 
     def strip(half):
-        return pl.ds(half * height, height)
+        return strips[half]
 
     def pair_sends(step):
         block, half = steps[step]
@@ -270,21 +288,31 @@
             for peer in others(my_inner, inner)
         ]
 
+    for step, block in enumerate(order):
+        for peer in others(my_inner, inner):
+            pack(near_sums, strips[0], block * inner + peer)
+        for copy in pair_sends(step):
+            copy.start()
+    for part in range(PARTS):
+        for peer in far:
+            block = mate_of(peer)
+            arrived(far_piece(block, part, col), recv_sem.at[block, part])
+    products(far_ref, far_sums, 0, chunks, jnp.zeros((width - near, side), jnp.float32))
     for index, block in enumerate(order):
         for peer in others(my_inner, inner):
-            pack(block * inner + peer)
-        if index == 0:
-            for step in range(2):
-                for copy in pair_sends(step):
-                    copy.start()
+            pack(far_sums, strips[1], block * inner + peer)
+        if index < 2:
+            for copy in pair_sends(outer + index):
+                copy.start()
     for block in order:
-        pack(block * inner + my_inner)
+        pack(near_sums, strips[0], block * inner + my_inner)
+        pack(far_sums, strips[1], block * inner + my_inner)
     values = []
-    grads = [0.0] * HALVES
+    grads = [0.0] * 2
     for step, (block, half) in enumerate(steps):
         for copy in pair_sends(step):
             copy.wait_send()
-        if step + 2 < len(steps):
+        if outer <= step < len(steps) - 2:
             for copy in pair_sends(step + 2):
                 copy.start()
         value = part_ref[block * inner + my_inner, strip(half)].astype(jnp.float32)
@@ -308,7 +336,12 @@
             if half == 0:
                 arrived(feat_ref.at[block], feat_recv_sem.at[block])
         grads[half] += jnp.dot(rounded, feat_ref[block], preferred_element_type=jnp.float32)
-    local_grad[...] = jnp.concatenate(grads, axis=0).T
+    turned = jnp.concatenate(grads, axis=0)
+    for position in range(cols):
+        whole_grad[lines_of(lax.rem(position + first, cols)), :] = turned[
+            position * own_width : (position + 1) * own_width
+        ]
+    local_grad[...] = whole_grad[...].T
     piece = local_grad.shape[0] // cols
 
     def rows_of(ref, index):
@@ -339,13 +372,17 @@
                 (peer, col),
             )
         )
-    for half in range(HALVES):
+    for half in range(2):
         for peer in reversed(order[:-1]):
             arrived(line_recv.at[peer, strip(half)], line_recv_sem.at[peer, half])
             values[half] += line_recv[peer, strip(half)].astype(jnp.float32)
-    aggregate = jnp.concatenate(values, axis=0).astype(jnp.bfloat16)
+    turned = jnp.concatenate(values, axis=0).astype(jnp.bfloat16)
+    for position in range(cols):
+        aggregate[lines_of(lax.rem(position + first, cols)), :] = turned[
+            position * own_width : (position + 1) * own_width
+        ]
     node_out_ref[...] = (
-        jnp.dot(weight_ref[...], aggregate, preferred_element_type=jnp.float32)
+        jnp.dot(weight_ref[...], aggregate[...], preferred_element_type=jnp.float32)
         .T.astype(jnp.bfloat16)
     )
     node_store = pltpu.make_async_copy(node_out_ref, node_out_hbm, store_sem.at[0])
@@ -437,13 +474,15 @@
         scratch_shapes=[
             pltpu.VMEM((own_width, block_nodes), bf16),
             pltpu.VMEM((own_width, block_nodes), i32),
-            pltpu.VMEM((block_nodes // side, width, side), bf16),
+            pltpu.VMEM((block_nodes // side, 2 * own_width, side), bf16),
+            pltpu.VMEM((block_nodes // side, width - 2 * own_width, side), bf16),
             pltpu.VMEM((slots, side, side), bf16),
             pltpu.VMEM((1, slots), i32),
             pltpu.VMEM((1, slots), i32),
             pltpu.VMEM((8, slots), i32),
             pltpu.SMEM((8, slots), i32),
-            pltpu.VMEM((slots, width, side), bf16),
+            pltpu.VMEM((slots, 2 * own_width, side), bf16),
+            pltpu.VMEM((slots, width - 2 * own_width, side), bf16),
             pltpu.VMEM((rows, width, nodes), bf16),
             pltpu.VMEM((outer, nodes, depth), bf16),
             pltpu.VMEM((depth, width), bf16),
@@ -455,6 +494,7 @@
             pltpu.VMEM((cols, piece, width), f32),
             pltpu.VMEM((rows, piece, width), bf16),
             pltpu.VMEM((depth, width), f32),
+            pltpu.VMEM((width, nodes), bf16),
             dma((6,)),
             dma((slots // CHUNK,)),
             dma((1,)),
@@ -462,10 +502,10 @@
             dma((cols, PARTS)),
             dma((cols, PARTS)),
             dma((cols, PARTS)),
-            dma((inner, outer, HALVES)),
-            dma((inner, outer, HALVES)),
-            dma((outer, HALVES)),
-            dma((outer, HALVES)),
+            dma((inner, outer, 2)),
+            dma((inner, outer, 2)),
+            dma((outer, 2)),
+            dma((outer, 2)),
             dma((cols,)),
             dma((cols,)),
             dma((rows,)),

time: 44.2 us -> 41.4 us (0.937)
  Pallas kernels: 42.7 us -> 39.9 us
    pallas_call x1, Pallas kernels: 41.1 us -> 38.3 us  [local(): pl.pallas_call(functools.partial(layer_kernel, outer, inner, cols), out_s...]
where the time goes in v5:
time: 41.4 us; the launch traced here: 41.2 us
  Pallas kernels  39.9 us (96%)
  between operations  1.29 us (3%)
    pallas_call x1, Pallas kernels, local(): pl.pallas_call(functools.partial(layer_kernel, outer, inner, cols), out_s...  38.3 us
    pallas_call x1, Pallas kernels, local(): pl.pallas_call(finish_kernel, out_shape=(jax.ShapeDtypeStruct((nodes, dep...  1.66 us

profile of v5, /device:TPU:0, one launch (start us, length us, event | category | flops | bytes accessed | tf_op | source)
XLA Modules:
  0.0 41.2 jit_solution(1223990188211308239)
XLA Ops:
  1.3 38.3 %layer_backward.1 = (bf16[512,128]{1,0:T(8,128)(2,1)}, f32[128,128]{1,0:T(8,128)}) custom-call(s32[1,256]{1,0:T(1,128)} %bitcast.8, s32[1,256]{1,0:T(1,128)} %bitcast.9, s32[1,1]{1,0:T(1,128)S(6)} %copy.12.count_ref, bf16[32,2048]{1,0:T(8,128)(2,1)} %bitcast.7, s32[32,2048]{1,0:T(8,128)} %bitcast.6, bf16[256,128,128]{2,1,0:T(8,128)(2,1)} %bitcast.5, ...), custom_call_target="tpu_custom_call" | custom-call | tf_op jit(solution)/shard_map/layer_backward/pallas_call | solution.py:466
  39.6 1.7 %finish.1 = (bf16[512,128]{1,0:T(8,128)(2,1)}, f32[128,128]{1,0:T(8,128)}) custom-call(bf16[512,128]{1,0:T(8,128)(2,1)} %get-tuple-element.4.node_hbm, f32[128,128]{1,0:T(8,128)} %get-tuple-element.5.grad_hbm, f32[128,128]{1,0:T(8,128)} %imp_hbm.1, f32[128,128]{1,0:T(8,128)} %delta_hbm.1), custom_call_target="tpu_custom_call" | custom-call | tf_op jit(solution)/shard_map/finish/pallas_call | solution.py:531

commit v6 on v5

--- a/solution.py
+++ b/solution.py
@@ -116,6 +116,7 @@
     all_recv_sem,
     feat_send_sem,
     feat_recv_sem,
+    hand_sem,
 ):
     row, col = lax.axis_index("row"), lax.axis_index("col")
     rows = outer * inner
@@ -135,8 +136,10 @@
 
     if outer == 4:
         across = lax.rem(my_outer + 2, outer)
-        order = [across, mate_of(across), mate_of(my_outer), my_outer]
+        outer_mate = mate_of(my_outer)
+        order = [across, mate_of(across), outer_mate, my_outer]
     else:
+        outer_mate = None
         order = others(my_outer, outer) + [my_outer]
 
     loads = [
@@ -217,7 +220,10 @@
             )
         ref = near_piece(col, part)
         start(remote(ref, ref, send_sem.at[mate, part], recv_sem.at[col, part], (row, mate)))
-    for peer in order[:-1]:
+    line = outer == 4
+    near_end = lax.div(lax.rem(my_outer + 1, 4), 2)
+    nearer = 2 - lax.div(my_outer, 2)
+    for peer in [nearer, mate_of(my_outer)] if line else order[:-1]:
         start(
             remote(
                 feat_hbm,
@@ -297,7 +303,28 @@
         for peer in far:
             block = mate_of(peer)
             arrived(far_piece(block, part, col), recv_sem.at[block, part])
-    products(far_ref, far_sums, 0, chunks, jnp.zeros((width - near, side), jnp.float32))
+    zeros = jnp.zeros((width - near, side), jnp.float32)
+    running = products(far_ref, far_sums, 0, chunks // 2, zeros)
+
+    def hand_on(block):
+        return remote(
+            feat_ref.at[block],
+            feat_ref.at[block],
+            hand_sem.at[block],
+            feat_recv_sem.at[block],
+            (mate_of(my_outer) * inner + my_inner, col),
+        )
+
+    other_pair = [2 * (1 - lax.div(my_outer, 2)), 2 * (1 - lax.div(my_outer, 2)) + 1]
+    if line:
+
+        @pl.when(near_end == 1)
+        def _():
+            for block in other_pair:
+                arrived(feat_ref.at[block], feat_recv_sem.at[block])
+                hand_on(block).start()
+
+    products(far_ref, far_sums, chunks // 2, chunks, running)
     for index, block in enumerate(order):
         for peer in others(my_inner, inner):
             pack(far_sums, strips[1], block * inner + peer)
@@ -308,6 +335,7 @@
         pack(near_sums, strips[0], block * inner + my_inner)
         pack(far_sums, strips[1], block * inner + my_inner)
     values = []
+    near_pairs = []
     grads = [0.0] * 2
     for step, (block, half) in enumerate(steps):
         for copy in pair_sends(step):
@@ -333,9 +361,20 @@
                     (block * inner + my_inner, col),
                 )
             )
-            if half == 0:
+        if half == 0:
+            near_pairs.append(rounded)
+            continue
+        if block is not my_outer:
+            if line and block is not outer_mate:
+
+                @pl.when(near_end == 0)
+                def _(block=block):
+                    arrived(feat_ref.at[block], feat_recv_sem.at[block])
+
+            else:
                 arrived(feat_ref.at[block], feat_recv_sem.at[block])
-        grads[half] += jnp.dot(rounded, feat_ref[block], preferred_element_type=jnp.float32)
+        for index, pairs in enumerate([near_pairs[step - outer], rounded]):
+            grads[index] += jnp.dot(pairs, feat_ref[block], preferred_element_type=jnp.float32)
     turned = jnp.concatenate(grads, axis=0)
     for position in range(cols):
         whole_grad[lines_of(lax.rem(position + first, cols)), :] = turned[
@@ -409,6 +448,13 @@
     weight_store.start()
     for copy in sends:
         copy.wait_send()
+    if line:
+
+        @pl.when(near_end == 1)
+        def _():
+            for block in other_pair:
+                hand_on(block).wait_send()
+
     node_store.wait()
     weight_store.wait()
 
@@ -514,6 +560,7 @@
             dma((cols,)),
             dma((outer,)),
             dma((outer,)),
+            dma((outer,)),
         ],
         compiler_params=params(collective_id=0, has_side_effects=True),
         name="layer_backward",

time: 41.4 us -> 45 us (1.087)
  Pallas kernels: 39.9 us -> 43.6 us
    pallas_call x1, Pallas kernels: 38.3 us -> 41.9 us  [local(): pl.pallas_call(functools.partial(layer_kernel, outer, inner, cols), out_s...]
where the time goes in v6:
time: 45 us; the launch traced here: 44.8 us
  Pallas kernels  43.6 us (97%)
  between operations  1.29 us (3%)
    pallas_call x1, Pallas kernels, local(): pl.pallas_call(functools.partial(layer_kernel, outer, inner, cols), out_s...  41.9 us
    pallas_call x1, Pallas kernels, local(): pl.pallas_call(finish_kernel, out_shape=(jax.ShapeDtypeStruct((nodes, dep...  1.66 us

profile of v6, /device:TPU:0, one launch (start us, length us, event | category | flops | bytes accessed | tf_op | source)
XLA Modules:
  0.0 44.8 jit_solution(10148287550511211895)
XLA Ops:
  1.3 41.9 %layer_backward.1 = (bf16[512,128]{1,0:T(8,128)(2,1)}, f32[128,128]{1,0:T(8,128)}) custom-call(s32[1,256]{1,0:T(1,128)} %bitcast.8, s32[1,256]{1,0:T(1,128)} %bitcast.9, s32[1,1]{1,0:T(1,128)S(6)} %copy.12.count_ref, bf16[32,2048]{1,0:T(8,128)(2,1)} %bitcast.7, s32[32,2048]{1,0:T(8,128)} %bitcast.6, bf16[256,128,128]{2,1,0:T(8,128)(2,1)} %bitcast.5, ...), custom_call_target="tpu_custom_call" | custom-call | tf_op jit(solution)/shard_map/layer_backward/pallas_call | solution.py:512
  43.2 1.7 %finish.1 = (bf16[512,128]{1,0:T(8,128)(2,1)}, f32[128,128]{1,0:T(8,128)}) custom-call(bf16[512,128]{1,0:T(8,128)(2,1)} %get-tuple-element.4.node_hbm, f32[128,128]{1,0:T(8,128)} %get-tuple-element.5.grad_hbm, f32[128,128]{1,0:T(8,128)} %imp_hbm.1, f32[128,128]{1,0:T(8,128)} %delta_hbm.1), custom_call_target="tpu_custom_call" | custom-call | tf_op jit(solution)/shard_map/finish/pallas_call | solution.py:578

commit v7 on v5

--- a/solution.py
+++ b/solution.py
@@ -308,6 +308,7 @@
         pack(near_sums, strips[0], block * inner + my_inner)
         pack(far_sums, strips[1], block * inner + my_inner)
     values = []
+    near_pairs = []
     grads = [0.0] * 2
     for step, (block, half) in enumerate(steps):
         for copy in pair_sends(step):
@@ -333,9 +334,13 @@
                     (block * inner + my_inner, col),
                 )
             )
-            if half == 0:
-                arrived(feat_ref.at[block], feat_recv_sem.at[block])
-        grads[half] += jnp.dot(rounded, feat_ref[block], preferred_element_type=jnp.float32)
+        if half == 0:
+            near_pairs.append(rounded)
+            continue
+        if block is not my_outer:
+            arrived(feat_ref.at[block], feat_recv_sem.at[block])
+        for index, pairs in enumerate([near_pairs[step - outer], rounded]):
+            grads[index] += jnp.dot(pairs, feat_ref[block], preferred_element_type=jnp.float32)
     turned = jnp.concatenate(grads, axis=0)
     for position in range(cols):
         whole_grad[lines_of(lax.rem(position + first, cols)), :] = turned[

time: 41.4 us -> 41.4 us (level)
  no operation moved by 1% of the time
where the time goes in v7:
time: 41.4 us; the launch traced here: 41.2 us
  Pallas kernels  39.9 us (96%)
  between operations  1.29 us (3%)
    pallas_call x1, Pallas kernels, local(): pl.pallas_call(functools.partial(layer_kernel, outer, inner, cols), out_s...  38.3 us
    pallas_call x1, Pallas kernels, local(): pl.pallas_call(finish_kernel, out_shape=(jax.ShapeDtypeStruct((nodes, dep...  1.66 us

profile of v7, /device:TPU:0, one launch (start us, length us, event | category | flops | bytes accessed | tf_op | source)
XLA Modules:
  0.0 41.2 jit_solution(2112107437507142818)
XLA Ops:
  1.3 38.3 %layer_backward.1 = (bf16[512,128]{1,0:T(8,128)(2,1)}, f32[128,128]{1,0:T(8,128)}) custom-call(s32[1,256]{1,0:T(1,128)} %bitcast.8, s32[1,256]{1,0:T(1,128)} %bitcast.9, s32[1,1]{1,0:T(1,128)S(6)} %copy.12.count_ref, bf16[32,2048]{1,0:T(8,128)(2,1)} %bitcast.7, s32[32,2048]{1,0:T(8,128)} %bitcast.6, bf16[256,128,128]{2,1,0:T(8,128)(2,1)} %bitcast.5, ...), custom_call_target="tpu_custom_call" | custom-call | tf_op jit(solution)/shard_map/layer_backward/pallas_call | solution.py:471
  39.6 1.7 %finish.1 = (bf16[512,128]{1,0:T(8,128)(2,1)}, f32[128,128]{1,0:T(8,128)}) custom-call(bf16[512,128]{1,0:T(8,128)(2,1)} %get-tuple-element.4.node_hbm, f32[128,128]{1,0:T(8,128)} %get-tuple-element.5.grad_hbm, f32[128,128]{1,0:T(8,128)} %imp_hbm.1, f32[128,128]{1,0:T(8,128)} %delta_hbm.1), custom_call_target="tpu_custom_call" | custom-call | tf_op jit(solution)/shard_map/finish/pallas_call | solution.py:536
